TPU v7x, 32 devices: a whole 2x2x4 slice. The times are simulated.
32 devices in a mesh: dp: 4 (over y, x), fsdp: 8 (over z, core).
Axes of the slice: x: 2, y: 2, z: 4, core: 2. Of those that a mesh axis runs over, the one named last changes fastest.
Arguments:
- tokens: bfloat16 [4096, 3072], P(('dp', 'fsdp')), may hold values from -6 to 6
- hess_tokens: bfloat16 [1024, 3072], P(('dp', 'fsdp')), may hold values from -6 to 6
- upstream: bfloat16 [4096, 12288], P('dp', 'fsdp'), may hold values from -5 to 5
- hess_upstream: bfloat16 [1024, 12288], P('dp', 'fsdp'), may hold values from -0.75 to 0.75
- weight: bfloat16 [3072, 12288], P(None, 'fsdp'), may hold values from -0.109375 to 0.109375
- probes: bfloat16 [3072, 12288], P('dp', 'fsdp'), may hold values from -6 to 6
- momentum: float32 [3072, 12288], P('dp', 'fsdp'), may hold values from -0.3 to 0.3
- curvature: float32 [3072, 12288], P('dp', 'fsdp'), may hold values from 0.1 to 10
Outputs:
- new_weight: bfloat16 [3072, 12288], P('dp', 'fsdp')
- new_momentum: float32 [3072, 12288], P('dp', 'fsdp')
- new_curvature: float32 [3072, 12288], P('dp', 'fsdp')
All inputs are finite; a program needn't handle non-finite values.
Results may differ from a plain program's by a relative error of at most 0.015.
Values may be sent and summed in bfloat16 or wider, within the bound.
A program may use at most 128 MiB of HBM per device.

v0:
```python
import math

import jax
import jax.numpy as jnp
from jax import lax
from jax.sharding import PartitionSpec as P

SQRT_HALF = 1.0 / math.sqrt(2.0)
INV_ROOT_TAU = 1.0 / math.sqrt(2.0 * math.pi)
BETA_ONE = 0.965
BETA_TWO = 0.99
LEARN_RATE = 0.0006
WEIGHT_DECAY = 0.1
HESS_SCALE = 0.01
RATIO_FLOOR = 0.001


def gelu_slope(preact):
    normal_cdf = 0.5 * (1.0 + jax.scipy.special.erf(preact * SQRT_HALF))
    density = jnp.exp(-0.5 * preact * preact) * INV_ROOT_TAU
    return normal_cdf + preact * density


def gelu_bend(preact):
    density = jnp.exp(-0.5 * preact * preact) * INV_ROOT_TAU
    return density * (2.0 - preact * preact)


def row_contract(left, right):
    return lax.dot_general(
        left, right, (((0,), (0,)), ((), ())), preferred_element_type=jnp.float32
    )


def grad_slopes(batch_rows, weight, signal):
    preact = jnp.dot(batch_rows, weight, preferred_element_type=jnp.float32)
    return (signal.astype(jnp.float32) * gelu_slope(preact)).astype(jnp.bfloat16)


def curv_values(hess_rows, weight, full_probes, hess_signal):
    hess_pre = jnp.dot(hess_rows, weight, preferred_element_type=jnp.float32)
    tangent = jnp.dot(hess_rows, full_probes, preferred_element_type=jnp.float32)
    return (hess_signal.astype(jnp.float32) * gelu_bend(hess_pre) * tangent).astype(jnp.bfloat16)


def shards(tokens, hess_tokens, upstream, hess_upstream, weight, probes, momentum, curvature):
    full_probes = lax.all_gather(probes, "dp", axis=0, tiled=True)
    all_tokens, all_hess = (
        lax.all_gather(tokens, "fsdp", axis=0, tiled=True),
        lax.all_gather(hess_tokens, "fsdp", axis=0, tiled=True),
    )
    gradient_share = row_contract(all_tokens, grad_slopes(all_tokens, weight, upstream))
    hessian_share = row_contract(
        all_hess, curv_values(all_hess, weight, full_probes, hess_upstream)
    )
    gradient, hessian_vec = (
        lax.psum_scatter(
            gradient_share.astype(jnp.bfloat16), "dp", scatter_dimension=0, tiled=True
        ).astype(jnp.float32),
        lax.psum_scatter(
            hessian_share.astype(jnp.bfloat16), "dp", scatter_dimension=0, tiled=True
        ).astype(jnp.float32),
    )
    owned_rows = weight.shape[0] // lax.axis_size("dp")
    first_row = lax.axis_index("dp") * owned_rows
    own_weight = lax.dynamic_slice_in_dim(weight, first_row, owned_rows, 0)
    new_curvature = BETA_TWO * curvature + (1.0 - BETA_TWO) * (
        probes.astype(jnp.float32) * hessian_vec
    )
    new_momentum = BETA_ONE * momentum + (1.0 - BETA_ONE) * gradient
    ratio = jnp.clip(new_momentum / jnp.maximum(HESS_SCALE * new_curvature, RATIO_FLOOR), -1.0, 1.0)
    new_weight = (
        own_weight.astype(jnp.float32) * (1.0 - LEARN_RATE * WEIGHT_DECAY) - LEARN_RATE * ratio
    ).astype(jnp.bfloat16)
    return (new_weight, new_momentum, new_curvature)


def solution(mesh):
    return jax.shard_map(
        shards,
        mesh=mesh,
        in_specs=(
            P(("dp", "fsdp"), None),
            P(("dp", "fsdp"), None),
            P("dp", "fsdp"),
            P("dp", "fsdp"),
            P(None, "fsdp"),
            P("dp", "fsdp"),
            P("dp", "fsdp"),
            P("dp", "fsdp"),
        ),
        out_specs=(P("dp", "fsdp"), P("dp", "fsdp"), P("dp", "fsdp")),
        check_vma=False,
    )
```

profile of v0, /device:TPU:0, one launch (start us, length us, event | category | flops | bytes accessed | tf_op | source)
XLA Modules:
  0.0 428.6 jit_solution(12816396575263700244)
XLA Ops:
  7.2 0.0 all-gather.4.cloned.1.call-start
  7.2 0.7 all-gather.4.cloned.1.call-update
  7.9 0.0 all-gather.6.cloned.1.call-start
  7.9 0.7 all-gather.6.cloned.1.call-update
  8.6 0.0 all-gather.8.cloned.1.call-start
  8.7 0.7 all-gather.8.cloned.1.call-update
  9.4 0.0 reduce-scatter.3.cloned.1.call-start
  9.4 67.7 %all-gather.4.cloned.1.call-done = bf16[1024,3072]{1,0:T(8,128)(2,1)} async-done(((bf16[128,3072]{1,0:T(8,128)(2,1)}), bf16[1024,3072]{1,0:T(8,128)(2,1)}) %all-gather.4.cloned.1.call-update) | async-done | bytes 6291472 | tf_op jit(solution)/shard_map/all_gather | solution.py:49
  77.1 31.0 %fusion = bf16[3072,1536]{0,1:T(8,128)(2,1)} fusion(bf16[1024,3072]{1,0:T(8,128)(2,1)} %all-gather.4.cloned.1.call-done, bf16[1024,1536]{1,0:T(8,128)(2,1)} %param.10, bf16[3072,1536]{1,0:T(8,128)(2,1)} %param.12), kind=kOutput, calls=%fused_computation.2 | convolution fusion | flops 19349372928 | bytes 28311552 | tf_op jit(solution)/shard_map/dot_general | solution.py:30
  108.1 0.0 reduce-scatter.3.cloned.1.call-update
  108.1 0.0 copy-start.4
  108.2 0.2 reduce-scatter.5.cloned.1.call-start
  108.4 0.0 all-gather.6.cloned.1.call-done
  108.4 0.0 copy-start.3
  108.4 9.5 %fusion.26 = f32[256,1536]{1,0:T(8,128)} fusion(bf16[256,3072]{1,0:T(8,128)(2,1)} %all-gather.6.cloned.1.call-done, bf16[3072,1536]{1,0:T(8,128)(2,1)} %param.12), kind=kOutput, calls=%fused_computation.33 | convolution fusion | flops 2415919104 | bytes 12582912 | tf_op jit(solution)/shard_map/dot_general | solution.py:41
  117.9 82.4 %all-gather.8.cloned.1.call-done = bf16[3072,1536]{1,0:T(8,128)(2,1)} async-done(((bf16[768,1536]{1,0:T(8,128)(2,1)}), bf16[3072,1536]{1,0:T(8,128)(2,1)}) %all-gather.8.cloned.1.call-update) | async-done | bytes 9437200 | tf_op jit(solution)/shard_map/all_gather | solution.py:47
  200.3 0.0 copy-done.4
  200.3 6.8 %fusion.14 = bf16[256,1536]{1,0:T(8,128)(2,1)S(1)} fusion(bf16[256,3072]{1,0:T(8,128)(2,1)S(1)} %copy-done.3, bf16[3072,1536]{1,0:T(8,128)(2,1)} %all-gather.8.cloned.1.call-done, f32[256,1536]{1,0:T(8,128)} %fusion.26, bf16[256,1536]{1,0:T(8,128)(2,1)S(1)} %copy-done.4), kind=kOutput, calls=%fused_computation.20 | convolution fusion | flops 2419851264 | bytes 14155776 | tf_op jit(solution)/shard_map/dot_general | solution.py:42
  207.0 5.5 %fusion.1 = bf16[3072,1536]{0,1:T(8,128)(2,1)} fusion(bf16[256,1536]{1,0:T(8,128)(2,1)S(1)} %fusion.14, bf16[256,3072]{1,0:T(8,128)(2,1)S(1)} %copy-done.3), kind=kOutput, calls=%fused_computation.3 | convolution fusion | flops 2420637696 | bytes 11796480 | tf_op jit(solution)/shard_map/dot_general | solution.py:30
  212.5 0.0 reduce-scatter.5.cloned.1.call-update
  212.5 1.6 copy-done
  214.2 2.5 copy.14
  216.7 1.9 constant_dynamic-slice_fusion
  218.5 2.4 copy.18
  221.0 6.1 %copy.12 = f32[768,1536]{0,1:T(8,128)} copy(f32[768,1536]{1,0:T(8,128)} %param.14) | data formatting | bytes 9437184 | tf_op args[6]
  227.0 6.2 %copy.13 = f32[768,1536]{0,1:T(8,128)} copy(f32[768,1536]{1,0:T(8,128)} %param.15) | data formatting | bytes 9437184 | tf_op args[7]
  233.3 65.0 %reduce-scatter.3.cloned.1.call-done = bf16[768,1536]{0,1:T(8,128)(2,1)} async-done(((bf16[3072,1536]{0,1:T(8,128)(2,1)}), bf16[768,1536]{0,1:T(8,128)(2,1)}) %reduce-scatter.3.cloned.1.call-update) | async-done | bytes 2359312 | tf_op jit(solution)/shard_map/reduce_scatter | solution.py:57
  298.3 98.0 %reduce-scatter.5.cloned.1.call-done = bf16[768,1536]{0,1:T(8,128)(2,1)} async-done(((bf16[3072,1536]{0,1:T(8,128)(2,1)}), bf16[768,1536]{0,1:T(8,128)(2,1)}) %reduce-scatter.5.cloned.1.call-update) | async-done | bytes 2359312 | tf_op jit(solution)/shard_map/reduce_scatter | solution.py:60
  396.2 11.2 %subtract_convert_fusion = (bf16[768,1536]{0,1:T(8,128)(2,1)}, f32[768,1536]{0,1:T(8,128)}, f32[768,1536]{0,1:T(8,128)}) fusion(bf16[768,1536]{0,1:T(8,128)(2,1)} %copy.18, bf16[768,1536]{0,1:T(8,128)(2,1)} %reduce-scatter.5.cloned.1.call-done, bf16[768,1536]{0,1:T(8,128)(2,1)S(1)} %copy-done.1, f32[768,1536]{0,1:T(8,128)} %copy.13, ...), kind=kLoop, calls=%fused_computation.11 | loop fusion | flops 22413312 | bytes 30670848 | tf_op jit(solution)/shard_map/convert_element_type | solution.py:74
  407.4 6.0 %copy.16 = f32[768,1536]{1,0:T(8,128)} copy(f32[768,1536]{0,1:T(8,128)} %get-tuple-element.8) | data formatting | bytes 9437184
  413.5 6.2 %copy.17 = f32[768,1536]{1,0:T(8,128)} copy(f32[768,1536]{0,1:T(8,128)} %get-tuple-element.7) | data formatting | bytes 9437184
  419.7 2.4 copy.15
  (6 shorter events, 0.0 us)
Async XLA Ops:
  7.2 70.0 %all-gather.4.cloned.1.call-start = ((), (), s32[]{:S(2)}) async-start(), calls=%async_computation.2 | async-start | bytes 7077888 | tf_op jit(solution)/shard_map/all_gather | solution.py:49
  7.9 100.5 %all-gather.6.cloned.1.call-start = ((), (), s32[]{:S(2)}) async-start(), calls=%async_computation.4 | async-start | bytes 1769472 | tf_op jit(solution)/shard_map/all_gather | solution.py:50
  8.6 191.6 %all-gather.8.cloned.1.call-start = ((), (), s32[]{:S(2)}) async-start(), calls=%async_computation.5 | async-start | bytes 11796480 | tf_op jit(solution)/shard_map/all_gather | solution.py:47
  9.4 288.9 %reduce-scatter.3.cloned.1.call-start = ((), (), s32[]{:S(2)}) async-start(), calls=%async_computation.3 | async-start | bytes 11796480 | tf_op jit(solution)/shard_map/reduce_scatter | solution.py:57
  108.1 92.1 %copy-start.4 = (bf16[256,1536]{1,0:T(8,128)(2,1)S(1)}, bf16[256,1536]{1,0:T(8,128)(2,1)}, u32[]{:S(2)}) copy-start(bf16[256,1536]{1,0:T(8,128)(2,1)} %param.11) | copy-start | bytes 2359300
  108.2 288.1 %reduce-scatter.5.cloned.1.call-start = ((), (), s32[]{:S(2)}) async-start(), calls=%async_computation.6 | async-start | bytes 11796480 | tf_op jit(solution)/shard_map/reduce_scatter | solution.py:60
  108.4 91.8 %copy-start.3 = (bf16[256,3072]{1,0:T(8,128)(2,1)S(1)}, bf16[256,3072]{1,0:T(8,128)(2,1)}, u32[]{:S(2)}) copy-start(bf16[256,3072]{1,0:T(8,128)(2,1)} %all-gather.6.cloned.1.call-done) | copy-start | bytes 4718596
  212.5 1.7 copy-start
  227.0 169.2 %copy-start.1 = (bf16[768,1536]{0,1:T(8,128)(2,1)S(1)}, bf16[768,1536]{0,1:T(8,128)(2,1)}, u32[]{:S(2)}) copy-start(bf16[768,1536]{0,1:T(8,128)(2,1)} %copy.14) | copy-start | bytes 7077892
  413.5 6.2 %copy-start.2 = (bf16[768,1536]{0,1:T(8,128)(2,1)S(1)}, bf16[768,1536]{0,1:T(8,128)(2,1)}, u32[]{:S(2)}) copy-start(bf16[768,1536]{0,1:T(8,128)(2,1)} %get-tuple-element.6) | copy-start | bytes 7077892
Sparse Core Ops, SparseCore 0:
  9.6 67.4 all-gather.3
  78.8 23.7 all-gather.5
  104.4 95.8 all-gather.7
  203.2 95.0 reduce-scatter.2
  301.2 94.9 reduce-scatter.4
where the time goes:
time: 429 us
  waiting for transfers between devices  315 us (73%)
  matrix products  52.7 us (12%)
  local copies, waits for them, and re-layouts  35.4 us (8%)
  between operations  13.8 us (3%)
  other arithmetic  11.2 us (3%)
    reduce_scatter x1, waiting for transfers between devices, shards(): lax.psum_scatter(hessian_share.astype(jnp.bfloat16), 'dp', scatter_dimens...  98 us
    all_gather x1, waiting for transfers between devices, shards(): full_probes = lax.all_gather(probes, 'dp', axis=0, tiled=True)  82.4 us
    all_gather x1, waiting for transfers between devices, shards(): lax.all_gather(tokens, 'fsdp', axis=0, tiled=True)  67.7 us
    reduce_scatter x1, waiting for transfers between devices, shards(): lax.psum_scatter(gradient_share.astype(jnp.bfloat16), 'dp', scatter_dimen...  65 us
    dot_general x2, matrix products, row_contract(): lax.dot_general(left, right, (((0,), (0,)), ((), ())), preferred_element_...  36.5 us
    unnamed x17, local copies, waits for them, and re-layouts  33.5 us
    convert_element_type x1, other arithmetic, shards(): new_weight = (own_weight.astype(jnp.float32) * (1.0 - LEARN_RATE * WEIGHT...  11.2 us
    dot_general x1, matrix products, curv_values(): hess_pre = jnp.dot(hess_rows, weight, preferred_element_type=jnp.float32)  9.47 us
  transfers between devices with their start and end apart: 5, of which 4 were waited for; matrix products, arithmetic and copies ran while one was open for 17% of the time, Pallas kernels for 0%

commit v1 on v0

v1 whole, which is shorter than its diff:
```python
import functools
import math

import jax
import jax.numpy as jnp
from jax import lax
from jax.experimental import pallas as pl
from jax.experimental.pallas import tpu as pltpu
from jax.sharding import PartitionSpec as P

SQRT_HALF = 1.0 / math.sqrt(2.0)
INV_ROOT_TAU = 1.0 / math.sqrt(2.0 * math.pi)
BETA_ONE = 0.965
BETA_TWO = 0.99
LEARN_RATE = 0.0006
WEIGHT_DECAY = 0.1
HESS_SCALE = 0.01
RATIO_FLOOR = 0.001
VMEM_BYTES = 48 * 1024 * 1024
F32, BF16 = jnp.float32, jnp.bfloat16


def gelu_slope(preact):
    normal_cdf = 0.5 * (1.0 + jax.scipy.special.erf(preact * SQRT_HALF))
    density = jnp.exp(-0.5 * preact * preact) * INV_ROOT_TAU
    return normal_cdf + preact * density


def gelu_bend(preact):
    density = jnp.exp(-0.5 * preact * preact) * INV_ROOT_TAU
    return density * (2.0 - preact * preact)


def row_contract(left, right):
    return lax.dot_general(left, right, (((0,), (0,)), ((), ())), preferred_element_type=F32)


def swap(value, axis, bit):
    count = lax.axis_size(axis)
    return lax.ppermute(value, axis, [(i, i ^ bit) for i in range(count)])


def bit_orders(count):
    bits = [1 << k for k in range(count.bit_length() - 1)]
    return bits, bits[::-1]


def scatter_terms(parts, bits):
    parts = {j: ([v] if j == 0 else v) for j, v in parts.items()}
    for at, bit in enumerate(bits):
        later = sum(bits[at + 1:])
        for j in sorted((j for j in parts if j & bit), key=lambda j: -(j & later)):
            arrived = swap(parts.pop(j), "dp", bit)
            if j == bit:
                parts[0] = parts[0] + [arrived]
            else:
                parts[j ^ bit] = (parts[j ^ bit].astype(F32) + arrived.astype(F32)).astype(BF16)
    return parts[0]


def gather_all(value, bits):
    held = {0: value}
    for bit in bits:
        held.update({j ^ bit: swap(v, "dp", bit) for j, v in list(held.items())})
    return held


def contract_body(count, owners_ref, *refs):
    total = row_contract(refs[0][...], refs[count][...])
    for k in range(1, count):
        total = total + row_contract(refs[k][...], refs[count + k][...])
    refs[2 * count][0] = total.astype(BF16)


def grad_blocks(owners, lefts, rights, owned, half, side):
    count, blocks = len(lefts), owners.shape[0]
    tile = math.gcd(owned, 384)
    per = owned // tile
    depth = lefts[0].shape[0]
    return pl.pallas_call(
        functools.partial(contract_body, count),
        grid_spec=pltpu.PrefetchScalarGridSpec(
            num_scalar_prefetch=1,
            grid=(blocks, per),
            in_specs=[pl.BlockSpec((depth, tile), lambda b, m, o: (0, o[b] * per + m))] * count
            + [pl.BlockSpec((depth, half), lambda b, m, o: (0, side))] * count,
            out_specs=pl.BlockSpec((1, tile, half), lambda b, m, o: (b, m, 0)),
        ),
        out_shape=jax.ShapeDtypeStruct((blocks, owned, half), BF16),
        compiler_params=pltpu.CompilerParams(vmem_limit_bytes=VMEM_BYTES),
        cost_estimate=pl.CostEstimate(
            flops=2 * blocks * owned * half * depth * count,
            bytes_accessed=2 * (blocks * owned * half + depth * count * (blocks * owned + half)),
            transcendentals=0,
        ),
    )(owners, *lefts, *rights)


def curvature_body(count, probes_ref, curv_ref, *refs):
    total = row_contract(refs[0][...], refs[count][...])
    for k in range(1, count):
        total = total + row_contract(refs[k][...], refs[count + k][...])
    refs[2 * count][...] = BETA_TWO * curv_ref[...] + (1.0 - BETA_TWO) * (
        probes_ref[...].astype(F32) * total
    )


def curvature_step(probes, curvature, lefts, rights):
    owned, width = probes.shape
    count, depth = len(lefts), lefts[0].shape[0]
    tile = math.gcd(owned, 128)
    rows = pl.BlockSpec((tile, width), lambda m: (m, 0))
    return pl.pallas_call(
        functools.partial(curvature_body, count),
        grid=(owned // tile,),
        in_specs=[rows, rows]
        + [pl.BlockSpec((depth, tile), lambda m: (0, m))] * count
        + [pl.BlockSpec((depth, width), lambda m: (0, 0))] * count,
        out_specs=rows,
        out_shape=jax.ShapeDtypeStruct((owned, width), F32),
        compiler_params=pltpu.CompilerParams(vmem_limit_bytes=VMEM_BYTES),
        cost_estimate=pl.CostEstimate(
            flops=2 * owned * width * depth * count, bytes_accessed=12 * owned * width, transcendentals=0
        ),
    )(probes, curvature, *lefts, *rights)


def update_body(terms, half, owner_ref, weight_ref, mom_ref, curv_ref, *refs):
    out_weight, out_mom = refs[2 * terms:]
    for side in range(2):
        cols = slice(side * half, (side + 1) * half)
        pieces = refs[side * terms:(side + 1) * terms]
        gradient = pieces[0][...].astype(F32)
        for piece in pieces[1:]:
            gradient = gradient + piece[...].astype(F32)
        new_mom = BETA_ONE * mom_ref[:, cols] + (1.0 - BETA_ONE) * gradient
        floor = jnp.maximum(HESS_SCALE * curv_ref[:, cols], RATIO_FLOOR)
        ratio = jnp.clip(new_mom / floor, -1.0, 1.0)
        out_mom[:, cols] = new_mom
        out_weight[:, cols] = (
            weight_ref[:, cols].astype(F32) * (1.0 - LEARN_RATE * WEIGHT_DECAY) - LEARN_RATE * ratio
        ).astype(BF16)


def update_step(owner, weight, momentum, new_curvature, first, second):
    owned, width = momentum.shape
    half, terms = width // 2, len(first)
    tile = math.gcd(owned, 128)
    per = owned // tile
    rows = pl.BlockSpec((tile, width), lambda m, o: (m, 0))
    return pl.pallas_call(
        functools.partial(update_body, terms, half),
        grid_spec=pltpu.PrefetchScalarGridSpec(
            num_scalar_prefetch=1,
            grid=(per,),
            in_specs=[pl.BlockSpec((tile, width), lambda m, o: (o[0] * per + m, 0)), rows, rows]
            + [pl.BlockSpec((tile, half), lambda m, o: (m, 0))] * (2 * terms),
            out_specs=[rows, rows],
        ),
        out_shape=[
            jax.ShapeDtypeStruct((owned, width), BF16),
            jax.ShapeDtypeStruct((owned, width), F32),
        ],
        compiler_params=pltpu.CompilerParams(vmem_limit_bytes=VMEM_BYTES),
        cost_estimate=pl.CostEstimate(
            flops=10 * owned * width, bytes_accessed=22 * owned * width, transcendentals=0
        ),
    )(owner, weight, momentum, new_curvature, *first, *second)


def shards(tokens, hess_tokens, upstream, hess_upstream, weight, probes, momentum, curvature):
    n_dp, n_fsdp = lax.axis_size("dp"), lax.axis_size("fsdp")
    own, lane = lax.axis_index("dp"), lax.axis_index("fsdp")
    owned, width = probes.shape
    half = width // 2
    forward, backward = bit_orders(n_dp)
    sides = ((0, forward), (1, backward))

    all_hess = lax.all_gather(hess_tokens, "fsdp", axis=0, tiled=True)
    columns = {
        j: lax.dynamic_slice_in_dim(all_hess, (own ^ j) * owned, owned, 1) for j in range(n_dp)
    }
    hess_cols = {0: columns[0]}
    for j in range(1, n_dp):
        hess_cols[j] = swap(columns[j], "dp", j)

    chips = n_fsdp // 2
    ring = [p for p in range(0, chips, 2)] + [p for p in range(1, chips, 2)][::-1]
    place = {p: k for k, p in enumerate(ring)}
    steps = [
        (2 * p + c, 2 * ring[(place[p] + 1) % chips] + c) for p in range(chips) for c in range(2)
    ]
    spot = jnp.zeros((), jnp.int32)
    for p in range(chips):
        spot = spot + jnp.where(lane // 2 == p, place[p], 0).astype(jnp.int32)
    token_rows = tokens.shape[0]
    held = tokens
    token_chunks, slope_chunks = [], []
    for k in range(chips):
        at = (spot - k) % chips
        origin = jnp.zeros((), jnp.int32)
        for p in range(chips):
            origin = origin + jnp.where(at == place[p], p, 0).astype(jnp.int32)
        other = swap(held, "fsdp", 1)
        first = jnp.where(lane % 2 == 0, held, other)
        second = jnp.where(lane % 2 == 0, other, held)
        chunk = jnp.concatenate([first, second], axis=0)
        signal = lax.dynamic_slice_in_dim(upstream, origin * 2 * token_rows, 2 * token_rows, 0)
        preact = jnp.dot(chunk, weight, preferred_element_type=F32)
        slope_chunks.append((signal.astype(F32) * gelu_slope(preact)).astype(BF16))
        token_chunks.append(chunk)
        if k < chips - 1:
            held = lax.ppermute(held, "fsdp", steps)

    tangents = {
        j: jnp.dot(hess_cols[j], probes, preferred_element_type=F32).astype(BF16)
        for j in range(n_dp)
    }
    tangent_sides = []
    for side, bits in sides:
        part = {j: v[:, side * half:(side + 1) * half] for j, v in tangents.items()}
        terms = scatter_terms(part, bits)
        tangent_sides.append(sum(t.astype(F32) for t in terms))
    hess_pre = jnp.dot(all_hess, weight, preferred_element_type=F32)
    curved_sides = []
    for side, bits in sides:
        cols = slice(side * half, (side + 1) * half)
        curved = (
            hess_upstream[:, cols].astype(F32) * gelu_bend(hess_pre[:, cols]) * tangent_sides[side]
        ).astype(BF16)
        curved_sides.append(gather_all(curved, bits))
    curved_all = [
        jnp.concatenate([curved_sides[0][j], curved_sides[1][j]], axis=1) for j in range(n_dp)
    ]
    new_curvature = curvature_step(
        probes, curvature, [hess_cols[j] for j in range(n_dp)], curved_all
    )

    grad_terms = []
    shares = []
    for side, bits in sides:
        out_list = [j for j in range(n_dp) if j & bits[0]]
        out_list.sort(key=lambda j: -(j & ~bits[0]))
        owners = jnp.stack([own ^ j for j in out_list]).astype(jnp.int32)
        sent = grad_blocks(owners, token_chunks, slope_chunks, owned, half, side)
        shares.append({j: sent[k] for k, j in enumerate(out_list)})
    for side, bits in sides:
        keep_list = [j for j in range(n_dp) if not j & bits[0]][::-1]
        owners = jnp.stack([own ^ j for j in keep_list]).astype(jnp.int32)
        kept = grad_blocks(owners, token_chunks, slope_chunks, owned, half, side)
        shares[side].update({j: kept[k] for k, j in enumerate(keep_list)})
        grad_terms.append(scatter_terms(shares[side], bits))

    new_weight, new_momentum = update_step(
        own.astype(jnp.int32).reshape((1,)), weight, momentum, new_curvature, *grad_terms
    )
    return (new_weight, new_momentum, new_curvature)


def solution(mesh):
    return jax.shard_map(
        shards,
        mesh=mesh,
        in_specs=(
            P(("dp", "fsdp"), None),
            P(("dp", "fsdp"), None),
            P("dp", "fsdp"),
            P("dp", "fsdp"),
            P(None, "fsdp"),
            P("dp", "fsdp"),
            P("dp", "fsdp"),
            P("dp", "fsdp"),
        ),
        out_specs=(P("dp", "fsdp"), P("dp", "fsdp"), P("dp", "fsdp")),
        check_vma=False,
    )
```

time: 429 us -> 287 us (0.67)
  waiting for transfers between devices: 315 us -> 141 us
  Pallas kernels: 0 us -> 43.2 us
  starting transfers between devices: 0.37 us -> 35.8 us
  matrix products: 52.7 us -> 27.5 us
  local copies, waits for them, and re-layouts: 35.4 us -> 12.5 us
    reduce_scatter x2 -> x0, waiting for transfers between devices: 163 us -> none  [the longest x1 98 us: shards(): lax.psum_scatter(hessian_share.astype(jnp.bfloat16), 'dp', scatter_dimens...]
    all_gather x3 -> x1, waiting for transfers between devices: 150 us -> 0.01 us  [shards(): all_hess = lax.all_gather(hess_tokens, 'fsdp', axis=0, tiled=True)]
    ppermute x0 -> x28, waiting for transfers between devices: none -> 141 us  [the longest x25 94.5 us: swap(): return lax.ppermute(value, axis, [(i, i ^ bit) for i in range(count)])]
    pallas_call x0 -> x6, Pallas kernels: none -> 43.2 us  [the longest x4 25.9 us: grad_blocks(): pl.pallas_call(functools.partial(contract_body, count), grid_spec=pltpu.P...]
    ppermute x0 -> x28, starting transfers between devices: none -> 35.7 us  [the longest x25 25.4 us: swap(): return lax.ppermute(value, axis, [(i, i ^ bit) for i in range(count)])]
    unnamed x17 -> x48, local copies, waits for them, and re-layouts: 33.5 us -> 3.42 us
    dot_general x4 -> x9, matrix products: 52.7 us -> 27.5 us  [the longest x4 17.9 us: shards(): preact = jnp.dot(chunk, weight, preferred_element_type=F32)]
    convert_element_type x1 -> x5, other arithmetic: 11.2 us -> 4.8 us  [the longest x4 2.84 us: scatter_terms(): (parts[j ^ bit].astype(F32) + arrived.astype(F32)).astype(BF16)]
  transfers between devices with their start and end apart: 5 -> 29, of which waited for: 4 -> 10; matrix products, arithmetic and copies ran while one was open for 17% -> 17% of each run, Pallas kernels for 0% -> 12%
where the time goes in v1:
time: 287 us; the launch traced here: 286 us
  waiting for transfers between devices  141 us (49%)
  Pallas kernels  43.2 us (15%)
  starting transfers between devices  35.8 us (12%)
  matrix products  27.5 us (10%)
  between operations  14.6 us (5%)
  local copies, waits for them, and re-layouts  12.5 us (4%)
  other arithmetic  11.6 us (4%)
    ppermute x25, waiting for transfers between devices, swap(): return lax.ppermute(value, axis, [(i, i ^ bit) for i in range(count)])  94.5 us
    ppermute x3, waiting for transfers between devices, shards(): held = lax.ppermute(held, 'fsdp', steps)  46.1 us
    pallas_call x4, Pallas kernels, grad_blocks(): pl.pallas_call(functools.partial(contract_body, count), grid_spec=pltpu.P...  25.9 us
    ppermute x25, starting transfers between devices, swap(): return lax.ppermute(value, axis, [(i, i ^ bit) for i in range(count)])  25.4 us
    dot_general x4, matrix products, shards(): preact = jnp.dot(chunk, weight, preferred_element_type=F32)  17.9 us
    ppermute x3, starting transfers between devices, shards(): held = lax.ppermute(held, 'fsdp', steps)  10.3 us
    pallas_call x1, Pallas kernels, update_step(): pl.pallas_call(functools.partial(update_body, terms, half), grid_spec=plt...  9.26 us
    pallas_call x1, Pallas kernels, curvature_step(): pl.pallas_call(functools.partial(curvature_body, count), grid=(owned // t...  8.12 us
  transfers between devices with their start and end apart: 29, of which 10 were waited for; matrix products, arithmetic and copies ran while one was open for 17% of the time, Pallas kernels for 12%

profile of v1, /device:TPU:0, one launch (start us, length us, event | category | flops | bytes accessed | tf_op | source)
XLA Modules:
  0.0 285.9 jit_solution(17317405003388045861)
XLA Ops:
  7.2 4.1 %collective-permute-start.16 = (bf16[128,3072]{1,0:T(8,128)(2,1)}, bf16[128,3072]{1,0:T(8,128)(2,1)S(1)}, u32[]{:S(2)}, u32[]{:S(2)}) collective-permute-start(bf16[128,3072]{1,0:T(8,128)(2,1)} %param.8), channel_id=1, source_target_pairs={{0,4},{1,5},{2,0},{3,1},{4,6},{5,7},{6,2},{7,3},{8,12},{9,13},{10,... | collective-permute-start | bytes 2359304 | tf_op jit(solution)/shard_map/ppermute | solution.py:213
  11.7 25.7 %collective-permute-done.16 = bf16[128,3072]{1,0:T(8,128)(2,1)S(1)} collective-permute-done((bf16[128,3072]{1,0:T(8,128)(2,1)}, bf16[128,3072]{1,0:T(8,128)(2,1)S(1)}, u32[]{:S(2)}, u32[]{:S(2)}) %collective-permute-start.16) | collective-permute-done | bytes 786464 | tf_op jit(solution)/shard_map/ppermute | solution.py:213
  37.4 3.3 %collective-permute-start.18 = (bf16[128,3072]{1,0:T(8,128)(2,1)S(1)}, bf16[128,3072]{1,0:T(8,128)(2,1)S(1)}, u32[]{:S(2)}, u32[]{:S(2)}) collective-permute-start(bf16[128,3072]{1,0:T(8,128)(2,1)S(1)} %collective-permute-done.16), channel_id=1, source_target_pairs={{0,4},{1,5},{2,0},{3,1},{4,6},{5,7},{6,2},{7,3},{8,12},{9,13},{10,... | collective-permute-start | bytes 2359304 | tf_op jit(solution)/shard_map/ppermute | solution.py:213
  42.1 6.8 %fusion.7.refs_4_ = bf16[256,1536]{1,0:T(8,128)(2,1)S(1)} fusion(bf16[1024,1536]{1,0:T(8,128)(2,1)S(1)} %copy-done.17, s32[]{:T(128)S(6)} %select_n.177, bf16[3072,1536]{1,0:T(8,128)(2,1)} %weight_ref.1, bf16[128,3072]{1,0:T(8,128)(2,1)S(1)} %get-tuple-element.20, bf16[128,3072]{1,0:T(8,128)(2,1)S(1)} %get-tuple-element.19), kind=kOutput, calls=%fused_computation.17 | convolution fusion | flops 2423390208 | bytes 12582916 | tf_op jit(solution)/shard_map/dot_general | solution.py:209
  49.0 9.2 %collective-permute-done.18 = bf16[128,3072]{1,0:T(8,128)(2,1)S(1)} collective-permute-done((bf16[128,3072]{1,0:T(8,128)(2,1)S(1)}, bf16[128,3072]{1,0:T(8,128)(2,1)S(1)}, u32[]{:S(2)}, u32[]{:S(2)}) %collective-permute-start.18) | collective-permute-done | bytes 786464 | tf_op jit(solution)/shard_map/ppermute | solution.py:213
  58.2 3.0 %collective-permute-start.20 = (bf16[128,3072]{1,0:T(8,128)(2,1)S(1)}, bf16[128,3072]{1,0:T(8,128)(2,1)}, u32[]{:S(2)}, u32[]{:S(2)}) collective-permute-start(bf16[128,3072]{1,0:T(8,128)(2,1)S(1)} %collective-permute-done.18), channel_id=1, source_target_pairs={{0,4},{1,5},{2,0},{3,1},{4,6},{5,7},{6,2},{7,3},{8,12},{9,13},{10,... | collective-permute-start | bytes 2359304 | tf_op jit(solution)/shard_map/ppermute | solution.py:213
  62.7 3.0 %fusion.13.refs_5_ = bf16[256,1536]{1,0:T(8,128)(2,1)S(1)} fusion(bf16[1024,1536]{1,0:T(8,128)(2,1)S(1)} %copy-done.17, s32[]{:T(128)S(6)} %select_n.182, bf16[3072,1536]{1,0:T(8,128)(2,1)S(1)} %bitcast.41, bf16[128,3072]{1,0:T(8,128)(2,1)S(1)} %get-tuple-element.18, bf16[128,3072]{1,0:T(8,128)(2,1)S(1)} %get-tuple-element.17), kind=kOutput, calls=%fused_computation.23 | convolution fusion | flops 2423390208 | bytes 12582916 | tf_op jit(solution)/shard_map/dot_general | solution.py:209
  65.7 11.2 %collective-permute-done.20 = bf16[128,3072]{1,0:T(8,128)(2,1)} collective-permute-done((bf16[128,3072]{1,0:T(8,128)(2,1)S(1)}, bf16[128,3072]{1,0:T(8,128)(2,1)}, u32[]{:S(2)}, u32[]{:S(2)}) %collective-permute-start.20) | collective-permute-done | bytes 786464 | tf_op jit(solution)/shard_map/ppermute | solution.py:213
  78.1 3.9 %fusion.19.refs_6_ = bf16[256,1536]{1,0:T(8,128)(2,1)} fusion(bf16[1024,1536]{1,0:T(8,128)(2,1)S(1)} %copy-done.17, s32[]{:T(128)S(6)} %select_n.187, bf16[3072,1536]{1,0:T(8,128)(2,1)S(1)} %bitcast.41, bf16[128,3072]{1,0:T(8,128)(2,1)S(1)} %get-tuple-element.16, bf16[128,3072]{1,0:T(8,128)(2,1)S(1)} %get-tuple-element.15), kind=kOutput, calls=%fused_computation.29 | convolution fusion | flops 2423390208 | bytes 12582916 | tf_op jit(solution)/shard_map/dot_general | solution.py:209
  82.0 2.4 constant_dynamic-slice_fusion
  84.4 2.3 collective-permute-start.2
  87.9 1.7 convolution_convert_fusion.3
  89.6 5.5 %fusion.43 = f32[256,1536]{1,0:T(8,128)S(1)} fusion(bf16[256,3072]{1,0:T(8,128)(2,1)S(1)} %copy-done.9, bf16[3072,1536]{1,0:T(8,128)(2,1)} %weight_ref.1), kind=kOutput, calls=%fused_computation.89 | convolution fusion | flops 2415919104 | bytes 12582912 | tf_op jit(solution)/shard_map/dot_general | solution.py:224
  97.0 1.8 pad_maximum_fusion.2
  98.9 4.2 %fusion.25.refs_7_ = bf16[256,1536]{1,0:T(8,128)(2,1)S(1)} fusion(bf16[1024,1536]{1,0:T(8,128)(2,1)} %param.10, s32[]{:T(128)S(6)} %select_n.192, bf16[3072,1536]{1,0:T(8,128)(2,1)S(1)} %bitcast.43, bf16[128,3072]{1,0:T(8,128)(2,1)S(1)} %get-tuple-element.14, bf16[128,3072]{1,0:T(8,128)(2,1)S(1)} %get-tuple-element.13), kind=kOutput, calls=%fused_computation.35 | convolution fusion | flops 2423390208 | bytes 12582916 | tf_op jit(solution)/shard_map/dot_general | solution.py:209
  103.1 6.5 %shard_map.107 = bf16[2,768,768]{2,1,0:T(8,128)(2,1)} custom-call(s32[2]{0:T(128)S(1)} %get-tuple-element.28.owners_ref, bf16[256,3072]{1,0:T(8,128)(2,1)S(1)} %get-tuple-element.29.refs_0_, bf16[256,3072]{1,0:T(8,128)(2,1)} %get-tuple-element.30.refs_1_, bf16[256,3072]{1,0:T(8,128)(2,1)} %get-tuple-element.31.refs_2_, ...), custom_call_target="tpu_custom_call" | custom-call | flops 2415919104 | bytes 7077888 | tf_op jit(solution)/shard_map/pallas_call | solution.py:80
  109.6 2.8 slice_bitcast_fusion
  118.9 6.5 %shard_map.105 = bf16[2,768,768]{2,1,0:T(8,128)(2,1)} custom-call(s32[2]{0:T(128)S(1)} %get-tuple-element.27.owners_ref, bf16[256,3072]{1,0:T(8,128)(2,1)S(1)} %get-tuple-element.29.refs_0_, bf16[256,3072]{1,0:T(8,128)(2,1)} %get-tuple-element.30.refs_1_, bf16[256,3072]{1,0:T(8,128)(2,1)} %get-tuple-element.31.refs_2_, ...), custom_call_target="tpu_custom_call" | custom-call | flops 2415919104 | bytes 7077888 | tf_op jit(solution)/shard_map/pallas_call | solution.py:80
  130.2 6.5 %shard_map.106 = bf16[2,768,768]{2,1,0:T(8,128)(2,1)} custom-call(s32[2]{0:T(128)S(1)} %pad_add_fusion.2.owners_ref, bf16[256,3072]{1,0:T(8,128)(2,1)S(1)} %get-tuple-element.29.refs_0_, bf16[256,3072]{1,0:T(8,128)(2,1)} %get-tuple-element.30.refs_1_, bf16[256,3072]{1,0:T(8,128)(2,1)} %get-tuple-element.31.refs_2_, ...), custom_call_target="tpu_custom_call" | custom-call | flops 2415919104 | bytes 7077888 | tf_op jit(solution)/shard_map/pallas_call | solution.py:80
  136.6 13.2 %collective-permute-done.7 = bf16[256,768]{1,0:T(8,128)(2,1)} collective-permute-done((bf16[256,768]{1,0:T(8,128)(2,1)}, bf16[256,768]{1,0:T(8,128)(2,1)}, u32[]{:S(2)}, u32[]{:S(2)}) %collective-permute-start.7) | collective-permute-done | bytes 393248 | tf_op jit(solution)/shard_map/ppermute | solution.py:40
  156.9 6.5 %shard_map.104 = bf16[2,768,768]{2,1,0:T(8,128)(2,1)} custom-call(s32[2]{0:T(128)S(1)} %pad_add_fusion.owners_ref, bf16[256,3072]{1,0:T(8,128)(2,1)S(1)} %get-tuple-element.29.refs_0_, bf16[256,3072]{1,0:T(8,128)(2,1)} %get-tuple-element.30.refs_1_, bf16[256,3072]{1,0:T(8,128)(2,1)} %get-tuple-element.31.refs_2_, ...), custom_call_target="tpu_custom_call" | custom-call | flops 2415919104 | bytes 7077888 | tf_op jit(solution)/shard_map/pallas_call | solution.py:80
  163.4 1.8 collective-permute-done.5
  165.2 2.0 fusion.31
  171.8 16.2 %collective-permute-done.23 = bf16[768,768]{1,0:T(8,128)(2,1)S(1)} collective-permute-done((bf16[768,768]{1,0:T(8,128)(2,1)}, bf16[768,768]{1,0:T(8,128)(2,1)S(1)}, u32[]{:S(2)}, u32[]{:S(2)}) %collective-permute-start.23) | collective-permute-done | bytes 1179680 | tf_op jit(solution)/shard_map/ppermute | solution.py:40
  188.0 1.6 collective-permute-start.25
  189.6 6.8 %collective-permute-done.9 = bf16[256,768]{1,0:T(8,128)(2,1)S(1)} collective-permute-done((bf16[256,768]{1,0:T(8,128)(2,1)S(1)}, bf16[256,768]{1,0:T(8,128)(2,1)S(1)}, u32[]{:S(2)}, u32[]{:S(2)}) %collective-permute-start.9) | collective-permute-done | bytes 393248 | tf_op jit(solution)/shard_map/ppermute | solution.py:40
  196.4 1.6 collective-permute-start.13
  200.5 4.3 %collective-permute-done.10 = bf16[256,768]{1,0:T(8,128)(2,1)S(1)} collective-permute-done((bf16[256,768]{1,0:T(8,128)(2,1)S(1)}, bf16[256,768]{1,0:T(8,128)(2,1)S(1)}, u32[]{:S(2)}, u32[]{:S(2)}) %collective-permute-start.10) | collective-permute-done | bytes 393248 | tf_op jit(solution)/shard_map/ppermute | solution.py:40
  206.5 18.8 %collective-permute-done.13 = bf16[256,768]{1,0:T(8,128)(2,1)S(1)} collective-permute-done((bf16[256,768]{1,0:T(8,128)(2,1)S(1)}, bf16[256,768]{1,0:T(8,128)(2,1)S(1)}, u32[]{:S(2)}, u32[]{:S(2)}) %collective-permute-start.13) | collective-permute-done | bytes 393248 | tf_op jit(solution)/shard_map/ppermute | solution.py:40
  227.0 33.5 %collective-permute-done.14 = bf16[256,768]{1,0:T(8,128)(2,1)S(1)} collective-permute-done((bf16[256,768]{1,0:T(8,128)(2,1)S(1)}, bf16[256,768]{1,0:T(8,128)(2,1)S(1)}, u32[]{:S(2)}, u32[]{:S(2)}) %collective-permute-start.14) | collective-permute-done | bytes 393248 | tf_op jit(solution)/shard_map/ppermute | solution.py:40
  260.6 8.1 %shard_map.103.curv_ref = f32[768,1536]{1,0:T(8,128)} custom-call(bf16[768,1536]{1,0:T(8,128)(2,1)} %probes_ref.1, f32[768,1536]{1,0:T(8,128)} %curv_ref.1, bf16[256,768]{1,0:T(8,128)(2,1)S(1)} %get-tuple-element.24.refs_0_, bf16[256,768]{1,0:T(8,128)(2,1)S(1)} %collective-permute-done.refs_1_, bf16[256,768]{1,0:T(8,128)(2,1)S(1)} %collective-permute-done.1.refs_2_, ...), custom_call_target="tpu_custom_call" | custom-call | flops 2415919104 | bytes 14155776 | tf_op jit(solution)/shard_map/pallas_call | solution.py:113
  269.8 9.3 %shard_map.108 = (bf16[768,1536]{1,0:T(8,128)(2,1)}, f32[768,1536]{1,0:T(8,128)}) custom-call(s32[1]{0:T(128)} %bitcast.owner_ref, bf16[3072,1536]{1,0:T(8,128)(2,1)} %weight_ref.1, f32[768,1536]{1,0:T(8,128)} %mom_ref.1, f32[768,1536]{1,0:T(8,128)} %shard_map.103.curv_ref, bf16[768,768]{1,0:T(8,128)(2,1)S(1)} %slice_bitcast_fusion.7.refs_0_, ...), custom_call_target="tpu_custom_call" | custom-call | flops 11796480 | bytes 25952256 | tf_op jit(solution)/shard_map/pallas_call | solution.py:151
  (118 shorter events, 37.4 us)
Async XLA Ops:
  7.2 74.8 %all-gather.2.cloned.1.call-start = ((), (), s32[]{:S(2)}) async-start(), calls=%async_computation | async-start | bytes 1769472 | tf_op jit(solution)/shard_map/all_gather | solution.py:179
  7.2 30.2 %collective-permute-start.16 = (bf16[128,3072]{1,0:T(8,128)(2,1)}, bf16[128,3072]{1,0:T(8,128)(2,1)S(1)}, u32[]{:S(2)}, u32[]{:S(2)}) collective-permute-start(bf16[128,3072]{1,0:T(8,128)(2,1)} %param.8), channel_id=1, source_target_pairs={{0,4},{1,5},{2,0},{3,1},{4,6},{5,7},{6,2},{7,3},{8,12},{9,13},{10,... | collective-permute-start | bytes 2359304 | tf_op jit(solution)/shard_map/ppermute | solution.py:213
  11.3 29.4 %collective-permute-start.15 = (bf16[128,3072]{1,0:T(8,128)(2,1)}, bf16[128,3072]{1,0:T(8,128)(2,1)S(1)}, u32[]{:S(2)}, u32[]{:S(2)}) collective-permute-start(bf16[128,3072]{1,0:T(8,128)(2,1)} %param.8), channel_id=1, source_target_pairs={{0,1},{1,0},{2,3},{3,2},{4,5},{5,4},{6,7},{7,6},{8,9},{9,8},{10,11... | collective-permute-start | bytes 2359304 | tf_op jit(solution)/shard_map/ppermute | solution.py:40
  11.7 30.4 %copy-start.17 = (bf16[1024,1536]{1,0:T(8,128)(2,1)S(1)}, bf16[1024,1536]{1,0:T(8,128)(2,1)}, u32[]{:S(2)}) copy-start(bf16[1024,1536]{1,0:T(8,128)(2,1)} %param.10) | copy-start | bytes 9437188
  37.4 20.8 %collective-permute-start.18 = (bf16[128,3072]{1,0:T(8,128)(2,1)S(1)}, bf16[128,3072]{1,0:T(8,128)(2,1)S(1)}, u32[]{:S(2)}, u32[]{:S(2)}) collective-permute-start(bf16[128,3072]{1,0:T(8,128)(2,1)S(1)} %collective-permute-done.16), channel_id=1, source_target_pairs={{0,4},{1,5},{2,0},{3,1},{4,6},{5,7},{6,2},{7,3},{8,12},{9,13},{10,... | collective-permute-start | bytes 2359304 | tf_op jit(solution)/shard_map/ppermute | solution.py:213
  40.7 20.5 %collective-permute-start.17 = (bf16[128,3072]{1,0:T(8,128)(2,1)S(1)}, bf16[128,3072]{1,0:T(8,128)(2,1)S(1)}, u32[]{:S(2)}, u32[]{:S(2)}) collective-permute-start(bf16[128,3072]{1,0:T(8,128)(2,1)S(1)} %collective-permute-done.16), channel_id=1, source_target_pairs={{0,1},{1,0},{2,3},{3,2},{4,5},{5,4},{6,7},{7,6},{8,9},{9,8},{10,11... | collective-permute-start | bytes 2359304 | tf_op jit(solution)/shard_map/ppermute | solution.py:40
  40.7 22.0 %slice-start = ((s8[9437184]{0:T(1024)(128)(4,1)}), s8[4194304]{0:T(1024)(128)(4,1)S(1)}, s32[]{:S(2)}) async-start(s8[9437184]{0:T(1024)(128)(4,1)} %bitcast.40), calls=%async_computation.1 | async-start | bytes 8388608
  58.2 18.7 %collective-permute-start.20 = (bf16[128,3072]{1,0:T(8,128)(2,1)S(1)}, bf16[128,3072]{1,0:T(8,128)(2,1)}, u32[]{:S(2)}, u32[]{:S(2)}) collective-permute-start(bf16[128,3072]{1,0:T(8,128)(2,1)S(1)} %collective-permute-done.18), channel_id=1, source_target_pairs={{0,4},{1,5},{2,0},{3,1},{4,6},{5,7},{6,2},{7,3},{8,12},{9,13},{10,... | collective-permute-start | bytes 2359304 | tf_op jit(solution)/shard_map/ppermute | solution.py:213
  61.2 15.7 %collective-permute-start.19 = (bf16[128,3072]{1,0:T(8,128)(2,1)S(1)}, bf16[128,3072]{1,0:T(8,128)(2,1)S(1)}, u32[]{:S(2)}, u32[]{:S(2)}) collective-permute-start(bf16[128,3072]{1,0:T(8,128)(2,1)S(1)} %collective-permute-done.18), channel_id=1, source_target_pairs={{0,1},{1,0},{2,3},{3,2},{4,5},{5,4},{6,7},{7,6},{8,9},{9,8},{10,11... | collective-permute-start | bytes 2359304 | tf_op jit(solution)/shard_map/ppermute | solution.py:40
  76.9 18.4 %collective-permute-start.21 = (bf16[128,3072]{1,0:T(8,128)(2,1)}, bf16[128,3072]{1,0:T(8,128)(2,1)}, u32[]{:S(2)}, u32[]{:S(2)}) collective-permute-start(bf16[128,3072]{1,0:T(8,128)(2,1)} %collective-permute-done.20), channel_id=1, source_target_pairs={{0,1},{1,0},{2,3},{3,2},{4,5},{5,4},{6,7},{7,6},{8,9},{9,8},{10,11... | collective-permute-start | bytes 2359304 | tf_op jit(solution)/shard_map/ppermute | solution.py:40
  84.4 29.3 %collective-permute-start.2 = (bf16[256,768]{1,0:T(8,128)(2,1)S(1)}, bf16[256,768]{1,0:T(8,128)(2,1)S(1)}, u32[]{:S(2)}, u32[]{:S(2)}) collective-permute-start(bf16[256,768]{1,0:T(8,128)(2,1)S(1)} %get-tuple-element.21), channel_id=1, source_target_pairs={{0,24},{8,16},{16,8},{24,0},{1,25},{9,17},{17,9},{25,1},{2,26},{10... | collective-permute-start | bytes 1179656 | tf_op jit(solution)/shard_map/ppermute | solution.py:40
  86.7 30.6 %collective-permute-start = (bf16[256,768]{1,0:T(8,128)(2,1)S(1)}, bf16[256,768]{1,0:T(8,128)(2,1)S(1)}, u32[]{:S(2)}, u32[]{:S(2)}) collective-permute-start(bf16[256,768]{1,0:T(8,128)(2,1)S(1)} %get-tuple-element.23), channel_id=1, source_target_pairs={{0,8},{8,0},{16,24},{24,16},{1,9},{9,1},{17,25},{25,17},{2,10},{10... | collective-permute-start | bytes 1179656 | tf_op jit(solution)/shard_map/ppermute | solution.py:40
  87.2 38.2 %collective-permute-start.1 = (bf16[256,768]{1,0:T(8,128)(2,1)}, bf16[256,768]{1,0:T(8,128)(2,1)S(1)}, u32[]{:S(2)}, u32[]{:S(2)}) collective-permute-start(bf16[256,768]{1,0:T(8,128)(2,1)} %get-tuple-element.22), channel_id=1, source_target_pairs={{0,16},{8,24},{16,0},{24,8},{1,17},{9,25},{17,1},{25,9},{2,18},{10... | collective-permute-start | bytes 1179656 | tf_op jit(solution)/shard_map/ppermute | solution.py:40
  112.4 58.3 %collective-permute-start.26 = (bf16[768,768]{1,0:T(8,128)(2,1)S(1)}, bf16[768,768]{1,0:T(8,128)(2,1)S(1)}, u32[]{:S(2)}, u32[]{:S(2)}) collective-permute-start(bf16[768,768]{1,0:T(8,128)(2,1)S(1)} %get-tuple-element.9), channel_id=1, source_target_pairs={{0,16},{8,24},{16,0},{24,8},{1,17},{9,25},{17,1},{25,9},{2,18},{10... | collective-permute-start | bytes 3538952 | tf_op jit(solution)/shard_map/ppermute | solution.py:40
  115.3 34.5 %collective-permute-start.7 = (bf16[256,768]{1,0:T(8,128)(2,1)}, bf16[256,768]{1,0:T(8,128)(2,1)}, u32[]{:S(2)}, u32[]{:S(2)}) collective-permute-start(bf16[256,768]{1,0:T(8,128)(2,1)} %get-tuple-element.26), channel_id=1, source_target_pairs={{0,16},{8,24},{16,0},{24,8},{1,17},{9,25},{17,1},{25,9},{2,18},{10... | collective-permute-start | bytes 1179656 | tf_op jit(solution)/shard_map/ppermute | solution.py:40
  116.0 36.2 %collective-permute-start.4 = (bf16[256,768]{1,0:T(8,128)(2,1)S(1)}, bf16[256,768]{1,0:T(8,128)(2,1)}, u32[]{:S(2)}, u32[]{:S(2)}) collective-permute-start(bf16[256,768]{1,0:T(8,128)(2,1)S(1)} %get-tuple-element.25), channel_id=1, source_target_pairs={{0,8},{8,0},{16,24},{24,16},{1,9},{9,1},{17,25},{25,17},{2,10},{10... | collective-permute-start | bytes 1179656 | tf_op jit(solution)/shard_map/ppermute | solution.py:40
  118.1 38.2 %collective-permute-start.3 = (bf16[256,768]{1,0:T(8,128)(2,1)S(1)}, bf16[256,768]{1,0:T(8,128)(2,1)}, u32[]{:S(2)}, u32[]{:S(2)}) collective-permute-start(bf16[256,768]{1,0:T(8,128)(2,1)S(1)} %slice.82), channel_id=1, source_target_pairs={{0,8},{8,0},{16,24},{24,16},{1,9},{9,1},{17,25},{25,17},{2,10},{10... | collective-permute-start | bytes 1179656 | tf_op jit(solution)/shard_map/ppermute | solution.py:40
  127.2 36.2 %collective-permute-start.6 = (bf16[256,768]{1,0:T(8,128)(2,1)S(1)}, bf16[256,768]{1,0:T(8,128)(2,1)}, u32[]{:S(2)}, u32[]{:S(2)}) collective-permute-start(bf16[256,768]{1,0:T(8,128)(2,1)S(1)} %slice.87), channel_id=1, source_target_pairs={{0,16},{8,24},{16,0},{24,8},{1,17},{9,25},{17,1},{25,9},{2,18},{10... | collective-permute-start | bytes 1179656 | tf_op jit(solution)/shard_map/ppermute | solution.py:40
  130.2 22.1 %copy-start.14 = (bf16[256,1536]{1,0:T(8,128)(2,1)S(1)}, bf16[256,1536]{1,0:T(8,128)(2,1)}, u32[]{:S(2)}) copy-start(bf16[256,1536]{1,0:T(8,128)(2,1)} %copy-done.13) | copy-start | bytes 2359300
  150.9 12.5 %collective-permute-start.8 = (bf16[256,768]{1,0:T(8,128)(2,1)S(1)}, bf16[256,768]{1,0:T(8,128)(2,1)S(1)}, u32[]{:S(2)}, u32[]{:S(2)}) collective-permute-start(bf16[256,768]{1,0:T(8,128)(2,1)S(1)} %add_convert_fusion), channel_id=1, source_target_pairs={{0,8},{8,0},{16,24},{24,16},{1,9},{9,1},{17,25},{25,17},{2,10},{10... | collective-permute-start | bytes 1179656 | tf_op jit(solution)/shard_map/ppermute | solution.py:40
  153.4 11.9 %collective-permute-start.5 = (bf16[256,768]{1,0:T(8,128)(2,1)S(1)}, bf16[256,768]{1,0:T(8,128)(2,1)S(1)}, u32[]{:S(2)}, u32[]{:S(2)}) collective-permute-start(bf16[256,768]{1,0:T(8,128)(2,1)S(1)} %add_convert_fusion.1), channel_id=1, source_target_pairs={{0,16},{8,24},{16,0},{24,8},{1,17},{9,25},{17,1},{25,9},{2,18},{10... | collective-permute-start | bytes 1179656 | tf_op jit(solution)/shard_map/ppermute | solution.py:40
  156.4 31.6 %collective-permute-start.23 = (bf16[768,768]{1,0:T(8,128)(2,1)}, bf16[768,768]{1,0:T(8,128)(2,1)S(1)}, u32[]{:S(2)}, u32[]{:S(2)}) collective-permute-start(bf16[768,768]{1,0:T(8,128)(2,1)} %get-tuple-element.11), channel_id=1, source_target_pairs={{0,8},{8,0},{16,24},{24,16},{1,9},{9,1},{17,25},{25,17},{2,10},{10... | collective-permute-start | bytes 3538952 | tf_op jit(solution)/shard_map/ppermute | solution.py:40
  167.2 29.2 %collective-permute-start.9 = (bf16[256,768]{1,0:T(8,128)(2,1)S(1)}, bf16[256,768]{1,0:T(8,128)(2,1)S(1)}, u32[]{:S(2)}, u32[]{:S(2)}) collective-permute-start(bf16[256,768]{1,0:T(8,128)(2,1)S(1)} %get-tuple-element.7), channel_id=1, source_target_pairs={{0,8},{8,0},{16,24},{24,16},{1,9},{9,1},{17,25},{25,17},{2,10},{10... | collective-permute-start | bytes 1179656 | tf_op jit(solution)/shard_map/ppermute | solution.py:40
  168.6 31.4 %collective-permute-start.11 = (bf16[256,768]{1,0:T(8,128)(2,1)S(1)}, bf16[256,768]{1,0:T(8,128)(2,1)S(1)}, u32[]{:S(2)}, u32[]{:S(2)}) collective-permute-start(bf16[256,768]{1,0:T(8,128)(2,1)S(1)} %get-tuple-element.7), channel_id=1, source_target_pairs={{0,16},{8,24},{16,0},{24,8},{1,17},{9,25},{17,1},{25,9},{2,18},{10... | collective-permute-start | bytes 1179656 | tf_op jit(solution)/shard_map/ppermute | solution.py:40
  170.2 28.1 %collective-permute-start.12 = (bf16[256,768]{1,0:T(8,128)(2,1)S(1)}, bf16[256,768]{1,0:T(8,128)(2,1)S(1)}, u32[]{:S(2)}, u32[]{:S(2)}) collective-permute-start(bf16[256,768]{1,0:T(8,128)(2,1)S(1)} %get-tuple-element.8), channel_id=1, source_target_pairs={{0,16},{8,24},{16,0},{24,8},{1,17},{9,25},{17,1},{25,9},{2,18},{10... | collective-permute-start | bytes 1179656 | tf_op jit(solution)/shard_map/ppermute | solution.py:40
  170.7 34.1 %collective-permute-start.10 = (bf16[256,768]{1,0:T(8,128)(2,1)S(1)}, bf16[256,768]{1,0:T(8,128)(2,1)S(1)}, u32[]{:S(2)}, u32[]{:S(2)}) collective-permute-start(bf16[256,768]{1,0:T(8,128)(2,1)S(1)} %get-tuple-element.8), channel_id=1, source_target_pairs={{0,8},{8,0},{16,24},{24,16},{1,9},{9,1},{17,25},{25,17},{2,10},{10... | collective-permute-start | bytes 1179656 | tf_op jit(solution)/shard_map/ppermute | solution.py:40
  188.0 80.7 %collective-permute-start.25 = (bf16[768,768]{1,0:T(8,128)(2,1)S(1)}, bf16[768,768]{1,0:T(8,128)(2,1)S(1)}, u32[]{:S(2)}, u32[]{:S(2)}) collective-permute-start(bf16[768,768]{1,0:T(8,128)(2,1)S(1)} %copy-done.11), channel_id=1, source_target_pairs={{0,16},{8,24},{16,0},{24,8},{1,17},{9,25},{17,1},{25,9},{2,18},{10... | collective-permute-start | bytes 3538952 | tf_op jit(solution)/shard_map/ppermute | solution.py:40
  196.4 28.9 %collective-permute-start.13 = (bf16[256,768]{1,0:T(8,128)(2,1)S(1)}, bf16[256,768]{1,0:T(8,128)(2,1)S(1)}, u32[]{:S(2)}, u32[]{:S(2)}) collective-permute-start(bf16[256,768]{1,0:T(8,128)(2,1)S(1)} %collective-permute-done.9), channel_id=1, source_target_pairs={{0,16},{8,24},{16,0},{24,8},{1,17},{9,25},{17,1},{25,9},{2,18},{10... | collective-permute-start | bytes 1179656 | tf_op jit(solution)/shard_map/ppermute | solution.py:40
  198.4 70.3 %collective-permute-start.22 = (bf16[768,768]{1,0:T(8,128)(2,1)S(1)}, bf16[768,768]{1,0:T(8,128)(2,1)S(1)}, u32[]{:S(2)}, u32[]{:S(2)}) collective-permute-start(bf16[768,768]{1,0:T(8,128)(2,1)S(1)} %copy-done.12), channel_id=1, source_target_pairs={{0,8},{8,0},{16,24},{24,16},{1,9},{9,1},{17,25},{25,17},{2,10},{10... | collective-permute-start | bytes 3538952 | tf_op jit(solution)/shard_map/ppermute | solution.py:40
  200.0 68.7 %collective-permute-start.27 = (bf16[768,768]{1,0:T(8,128)(2,1)S(1)}, bf16[768,768]{1,0:T(8,128)(2,1)S(1)}, u32[]{:S(2)}, u32[]{:S(2)}) collective-permute-start(bf16[768,768]{1,0:T(8,128)(2,1)S(1)} %fusion), channel_id=1, source_target_pairs={{0,8},{8,0},{16,24},{24,16},{1,9},{9,1},{17,25},{25,17},{2,10},{10... | collective-permute-start | bytes 3538952 | tf_op jit(solution)/shard_map/ppermute | solution.py:40
  204.8 63.9 %collective-permute-start.24 = (bf16[768,768]{1,0:T(8,128)(2,1)S(1)}, bf16[768,768]{1,0:T(8,128)(2,1)S(1)}, u32[]{:S(2)}, u32[]{:S(2)}) collective-permute-start(bf16[768,768]{1,0:T(8,128)(2,1)S(1)} %fusion.1), channel_id=1, source_target_pairs={{0,16},{8,24},{16,0},{24,8},{1,17},{9,25},{17,1},{25,9},{2,18},{10... | collective-permute-start | bytes 3538952 | tf_op jit(solution)/shard_map/ppermute | solution.py:40
  225.3 35.2 %collective-permute-start.14 = (bf16[256,768]{1,0:T(8,128)(2,1)S(1)}, bf16[256,768]{1,0:T(8,128)(2,1)S(1)}, u32[]{:S(2)}, u32[]{:S(2)}) collective-permute-start(bf16[256,768]{1,0:T(8,128)(2,1)S(1)} %collective-permute-done.12), channel_id=1, source_target_pairs={{0,8},{8,0},{16,24},{24,16},{1,9},{9,1},{17,25},{25,17},{2,10},{10... | collective-permute-start | bytes 1179656 | tf_op jit(solution)/shard_map/ppermute | solution.py:40
  (21 other events, 154.4 us)
Sparse Core Ops, SparseCore 0:
  11.4 34.0 all-gather.1

commit v2 on v1

--- a/solution.py
+++ b/solution.py
@@ -69,31 +69,30 @@
     total = row_contract(refs[0][...], refs[count][...])
     for k in range(1, count):
         total = total + row_contract(refs[k][...], refs[count + k][...])
-    refs[2 * count][0] = total.astype(BF16)
-
-
-def grad_blocks(owners, lefts, rights, owned, half, side):
-    count, blocks = len(lefts), owners.shape[0]
+    refs[2 * count][...] = total.astype(BF16)
+
+
+def grad_block(owner, lefts, rights, owned, half, side):
+    count, depth = len(lefts), lefts[0].shape[0]
     tile = math.gcd(owned, 384)
     per = owned // tile
-    depth = lefts[0].shape[0]
     return pl.pallas_call(
         functools.partial(contract_body, count),
         grid_spec=pltpu.PrefetchScalarGridSpec(
             num_scalar_prefetch=1,
-            grid=(blocks, per),
-            in_specs=[pl.BlockSpec((depth, tile), lambda b, m, o: (0, o[b] * per + m))] * count
-            + [pl.BlockSpec((depth, half), lambda b, m, o: (0, side))] * count,
-            out_specs=pl.BlockSpec((1, tile, half), lambda b, m, o: (b, m, 0)),
-        ),
-        out_shape=jax.ShapeDtypeStruct((blocks, owned, half), BF16),
+            grid=(per,),
+            in_specs=[pl.BlockSpec((depth, tile), lambda m, o: (0, o[0] * per + m))] * count
+            + [pl.BlockSpec((depth, half), lambda m, o: (0, side))] * count,
+            out_specs=pl.BlockSpec((tile, half), lambda m, o: (m, 0)),
+        ),
+        out_shape=jax.ShapeDtypeStruct((owned, half), BF16),
         compiler_params=pltpu.CompilerParams(vmem_limit_bytes=VMEM_BYTES),
         cost_estimate=pl.CostEstimate(
-            flops=2 * blocks * owned * half * depth * count,
-            bytes_accessed=2 * (blocks * owned * half + depth * count * (blocks * owned + half)),
+            flops=2 * owned * half * depth * count,
+            bytes_accessed=2 * (owned * half + depth * count * (owned + half)),
             transcendentals=0,
         ),
-    )(owners, *lefts, *rights)
+    )(owner.astype(jnp.int32).reshape((1,)), *lefts, *rights)
 
 
 def curvature_body(count, probes_ref, curv_ref, *refs):
@@ -176,13 +175,23 @@
     forward, backward = bit_orders(n_dp)
     sides = ((0, forward), (1, backward))
 
-    all_hess = lax.all_gather(hess_tokens, "fsdp", axis=0, tiled=True)
-    columns = {
-        j: lax.dynamic_slice_in_dim(all_hess, (own ^ j) * owned, owned, 1) for j in range(n_dp)
-    }
-    hess_cols = {0: columns[0]}
-    for j in range(1, n_dp):
-        hess_cols[j] = swap(columns[j], "dp", j)
+    hess_rows = hess_tokens.shape[0]
+    near = {0: hess_tokens}
+    for j in range(2, n_fsdp, 2):
+        near[j] = swap(hess_tokens, "fsdp", j)
+    chip_rows = jnp.concatenate([near[j] for j in range(0, n_fsdp, 2)], axis=0)
+    all_hess = jnp.concatenate([chip_rows, swap(chip_rows, "fsdp", 1)], axis=0)
+    order = [j for j in range(0, n_fsdp, 2)] + [j + 1 for j in range(0, n_fsdp, 2)]
+    hess_signal = jnp.concatenate(
+        [
+            lax.dynamic_slice_in_dim(hess_upstream, (lane ^ j) * hess_rows, hess_rows, 0)
+            for j in order
+        ],
+        axis=0,
+    )
+    columns = [
+        lax.dynamic_slice_in_dim(all_hess, (own ^ j) * owned, owned, 1) for j in range(n_dp)
+    ]
 
     chips = n_fsdp // 2
     ring = [p for p in range(0, chips, 2)] + [p for p in range(1, chips, 2)][::-1]
@@ -196,7 +205,17 @@
     token_rows = tokens.shape[0]
     held = tokens
     token_chunks, slope_chunks = [], []
+    tangents = None
     for k in range(chips):
+        if k == 1:
+            held, columns = lax.optimization_barrier((held, columns))
+            hess_cols = [columns[0]] + [swap(columns[j], "dp", j) for j in range(1, n_dp)]
+        later = lax.ppermute(held, "fsdp", steps) if k < chips - 1 else None
+        if k == 2:
+            tangents = [
+                jnp.dot(v, probes, preferred_element_type=F32).astype(BF16) for v in hess_cols
+            ]
+            held, tangents = lax.optimization_barrier((held, tangents))
         at = (spot - k) % chips
         origin = jnp.zeros((), jnp.int32)
         for p in range(chips):
@@ -209,47 +228,39 @@
         preact = jnp.dot(chunk, weight, preferred_element_type=F32)
         slope_chunks.append((signal.astype(F32) * gelu_slope(preact)).astype(BF16))
         token_chunks.append(chunk)
-        if k < chips - 1:
-            held = lax.ppermute(held, "fsdp", steps)
-
-    tangents = {
-        j: jnp.dot(hess_cols[j], probes, preferred_element_type=F32).astype(BF16)
-        for j in range(n_dp)
-    }
+        held = later
+
     tangent_sides = []
     for side, bits in sides:
-        part = {j: v[:, side * half:(side + 1) * half] for j, v in tangents.items()}
+        part = {j: v[:, side * half:(side + 1) * half] for j, v in enumerate(tangents)}
         terms = scatter_terms(part, bits)
         tangent_sides.append(sum(t.astype(F32) for t in terms))
     hess_pre = jnp.dot(all_hess, weight, preferred_element_type=F32)
-    curved_sides = []
+    curved_own, curved_sides = [], []
     for side, bits in sides:
         cols = slice(side * half, (side + 1) * half)
         curved = (
-            hess_upstream[:, cols].astype(F32) * gelu_bend(hess_pre[:, cols]) * tangent_sides[side]
+            hess_signal[:, cols].astype(F32) * gelu_bend(hess_pre[:, cols]) * tangent_sides[side]
         ).astype(BF16)
-        curved_sides.append(gather_all(curved, bits))
+        curved_own.append(curved)
+    curved_own, slope_chunks[-1] = lax.optimization_barrier((curved_own, slope_chunks[-1]))
+    for side, bits in sides:
+        curved_sides.append(gather_all(curved_own[side], bits))
     curved_all = [
         jnp.concatenate([curved_sides[0][j], curved_sides[1][j]], axis=1) for j in range(n_dp)
     ]
     new_curvature = curvature_step(
-        probes, curvature, [hess_cols[j] for j in range(n_dp)], curved_all
-    )
-
-    grad_terms = []
-    shares = []
-    for side, bits in sides:
-        out_list = [j for j in range(n_dp) if j & bits[0]]
-        out_list.sort(key=lambda j: -(j & ~bits[0]))
-        owners = jnp.stack([own ^ j for j in out_list]).astype(jnp.int32)
-        sent = grad_blocks(owners, token_chunks, slope_chunks, owned, half, side)
-        shares.append({j: sent[k] for k, j in enumerate(out_list)})
-    for side, bits in sides:
-        keep_list = [j for j in range(n_dp) if not j & bits[0]][::-1]
-        owners = jnp.stack([own ^ j for j in keep_list]).astype(jnp.int32)
-        kept = grad_blocks(owners, token_chunks, slope_chunks, owned, half, side)
-        shares[side].update({j: kept[k] for k, j in enumerate(keep_list)})
-        grad_terms.append(scatter_terms(shares[side], bits))
+        probes, curvature, hess_cols, curved_all
+    )
+
+    shares = [{}, {}]
+    for j in sorted(range(n_dp), key=lambda j: -j):
+        for side, bits in sides:
+            flip = sum(b for b, c in zip(bits[::-1], forward) if j & c)
+            shares[side][flip] = grad_block(
+                own ^ flip, token_chunks, slope_chunks, owned, half, side
+            )
+    grad_terms = [scatter_terms(shares[side], bits) for side, bits in sides]
 
     new_weight, new_momentum = update_step(
         own.astype(jnp.int32).reshape((1,)), weight, momentum, new_curvature, *grad_terms

time: 287 us -> 250 us (0.87)
  waiting for transfers between devices: 141 us -> 124 us
  between operations: 14.6 us -> 1.27 us
  matrix products: 27.5 us -> 21.7 us
  other arithmetic: 11.6 us -> 17.2 us
  local copies, waits for them, and re-layouts: 12.5 us -> 8.81 us
    ppermute x3, waiting for transfers between devices: 46.1 us -> 14.9 us  [shards(): later = lax.ppermute(held, 'fsdp', steps) if k < chips - 1 else None]
    ppermute x25 -> x29, waiting for transfers between devices: 94.5 us -> 109 us  [swap(): return lax.ppermute(value, axis, [(i, i ^ bit) for i in range(count)])]
    squeeze x4 -> x0, local copies, waits for them, and re-layouts: 5.83 us -> none  [the longest x2 4.41 us: shards(): shares.append({j: sent[k] for k, j in enumerate(out_list)})]
    unnamed x48 -> x33, local copies, waits for them, and re-layouts: 3.42 us -> 8.43 us
    ppermute x3, starting transfers between devices: 10.3 us -> 6.47 us  [shards(): later = lax.ppermute(held, 'fsdp', steps) if k < chips - 1 else None]
    ppermute x25 -> x29, starting transfers between devices: 25.4 us -> 29.1 us  [swap(): return lax.ppermute(value, axis, [(i, i ^ bit) for i in range(count)])]
    concatenate x4, other arithmetic: 0.21 us -> 3.31 us  [shards(): jnp.concatenate([curved_sides[0][j], curved_sides[1][j]], axis=1)]
    dot_general x1, matrix products: 5.55 us -> 2.59 us  [shards(): hess_pre = jnp.dot(all_hess, weight, preferred_element_type=F32)]
  transfers between devices with their start and end apart: 29 -> 32, of which waited for: 10 -> 11; matrix products, arithmetic and copies ran while one was open for 17% -> 17% of each run, Pallas kernels for 12% -> 11%
where the time goes in v2:
time: 250 us; the launch traced here: 249 us
  waiting for transfers between devices  124 us (50%)
  Pallas kernels  40.9 us (16%)
  starting transfers between devices  35.6 us (14%)
  matrix products  21.7 us (9%)
  other arithmetic  17.2 us (7%)
  local copies, waits for them, and re-layouts  8.81 us (4%)
    ppermute x29, waiting for transfers between devices, swap(): return lax.ppermute(value, axis, [(i, i ^ bit) for i in range(count)])  109 us
    ppermute x29, starting transfers between devices, swap(): return lax.ppermute(value, axis, [(i, i ^ bit) for i in range(count)])  29.1 us
    pallas_call x8, Pallas kernels, grad_block(): pl.pallas_call(functools.partial(contract_body, count), grid_spec=pltpu.P...  23.4 us
    dot_general x4, matrix products, shards(): preact = jnp.dot(chunk, weight, preferred_element_type=F32)  16 us
    ppermute x3, waiting for transfers between devices, shards(): later = lax.ppermute(held, 'fsdp', steps) if k < chips - 1 else None  14.9 us
    pallas_call x1, Pallas kernels, update_step(): pl.pallas_call(functools.partial(update_body, terms, half), grid_spec=plt...  9.32 us
    unnamed x33, local copies, waits for them, and re-layouts  8.43 us
    pallas_call x1, Pallas kernels, curvature_step(): pl.pallas_call(functools.partial(curvature_body, count), grid=(owned // t...  8.14 us
  transfers between devices with their start and end apart: 32, of which 11 were waited for; matrix products, arithmetic and copies ran while one was open for 17% of the time, Pallas kernels for 11%

profile of v2, /device:TPU:0, one launch (start us, length us, event | category | flops | bytes accessed | tf_op | source)
XLA Modules:
  0.0 249.0 jit_solution(7101335442604260751)
XLA Ops:
  0.7 3.1 %collective-permute-start.1 = (bf16[32,3072]{1,0:T(8,128)(2,1)}, bf16[32,3072]{1,0:T(8,128)(2,1)S(1)}, u32[]{:S(2)}, u32[]{:S(2)}) collective-permute-start(bf16[32,3072]{1,0:T(8,128)(2,1)} %param.9), channel_id=1, source_target_pairs={{0,2},{1,3},{2,0},{3,1},{4,6},{5,7},{6,4},{7,5},{8,10},{9,11},{10,... | collective-permute-start | bytes 589832 | tf_op jit(solution)/shard_map/ppermute | solution.py:40
  3.7 2.6 %collective-permute-start.2 = (bf16[32,3072]{1,0:T(8,128)(2,1)}, bf16[32,3072]{1,0:T(8,128)(2,1)}, u32[]{:S(2)}, u32[]{:S(2)}) collective-permute-start(bf16[32,3072]{1,0:T(8,128)(2,1)} %param.9), channel_id=1, source_target_pairs={{0,4},{1,5},{2,6},{3,7},{4,0},{5,1},{6,2},{7,3},{8,12},{9,13},{10,... | collective-permute-start | bytes 589832 | tf_op jit(solution)/shard_map/ppermute | solution.py:40
  6.3 1.9 collective-permute-start
  13.1 25.0 %collective-permute-done.2 = bf16[32,3072]{1,0:T(8,128)(2,1)} collective-permute-done((bf16[32,3072]{1,0:T(8,128)(2,1)}, bf16[32,3072]{1,0:T(8,128)(2,1)}, u32[]{:S(2)}, u32[]{:S(2)}) %collective-permute-start.2) | collective-permute-done | bytes 196640 | tf_op jit(solution)/shard_map/ppermute | solution.py:40
  43.3 6.9 %fusion.11.refs_4_ = bf16[256,1536]{1,0:T(8,128)(2,1)S(1)} fusion(bf16[1024,1536]{1,0:T(8,128)(2,1)S(1)} %copy-done.7, s32[]{:T(128)S(6)} %select_n.214, bf16[3072,1536]{1,0:T(8,128)(2,1)} %weight_ref.1, bf16[128,3072]{1,0:T(8,128)(2,1)S(1)} %get-tuple-element.40, bf16[128,3072]{1,0:T(8,128)(2,1)S(1)} %get-tuple-element.39), kind=kOutput, calls=%fused_computation.21 | convolution fusion | flops 2423390208 | bytes 12582916 | tf_op jit(solution)/shard_map/dot_general | solution.py:228
  50.6 4.4 %collective-permute-start.8 = (bf16[128,3072]{1,0:T(8,128)(2,1)}, bf16[128,3072]{1,0:T(8,128)(2,1)S(1)}, u32[]{:S(2)}, u32[]{:S(2)}) collective-permute-start(bf16[128,3072]{1,0:T(8,128)(2,1)} %collective-permute-done), channel_id=1, source_target_pairs={{0,4},{1,5},{2,0},{3,1},{4,6},{5,7},{6,2},{7,3},{8,12},{9,13},{10,... | collective-permute-start | bytes 2359304 | tf_op jit(solution)/shard_map/ppermute | solution.py:213
  55.2 2.4 collective-permute-start.7
  57.6 2.6 %fusion.41 = f32[256,1536]{1,0:T(8,128)S(1)} fusion(bf16[256,3072]{1,0:T(8,128)(2,1)S(1)} %constant_dynamic-update-slice_fusion, bf16[3072,1536]{1,0:T(8,128)(2,1)S(1)} %bitcast.19), kind=kOutput, calls=%fused_computation.89 | convolution fusion | flops 2415919104 | bytes 12582912 | tf_op jit(solution)/shard_map/dot_general | solution.py:238
  62.2 5.9 %collective-permute-done.7.refs_3_ = bf16[256,768]{1,0:T(8,128)(2,1)S(1)} collective-permute-done((bf16[256,768]{1,0:T(8,128)(2,1)S(1)}, bf16[256,768]{1,0:T(8,128)(2,1)S(1)}, u32[]{:S(2)}, u32[]{:S(2)}) %collective-permute-start.7) | collective-permute-done | bytes 393248 | tf_op jit(solution)/shard_map/ppermute | solution.py:40
  68.9 7.0 %collective-permute-done.6.refs_2_ = bf16[256,768]{1,0:T(8,128)(2,1)S(1)} collective-permute-done((bf16[256,768]{1,0:T(8,128)(2,1)S(1)}, bf16[256,768]{1,0:T(8,128)(2,1)S(1)}, u32[]{:S(2)}, u32[]{:S(2)}) %collective-permute-start.6) | collective-permute-done | bytes 393248 | tf_op jit(solution)/shard_map/ppermute | solution.py:40
  81.9 3.0 %fusion.17.refs_5_ = bf16[256,1536]{1,0:T(8,128)(2,1)S(1)} fusion(bf16[1024,1536]{1,0:T(8,128)(2,1)S(1)} %copy-done.7, s32[]{:T(128)S(6)} %select_n.219, bf16[3072,1536]{1,0:T(8,128)(2,1)S(1)} %bitcast.19, bf16[128,3072]{1,0:T(8,128)(2,1)S(1)} %get-tuple-element.38, bf16[128,3072]{1,0:T(8,128)(2,1)S(1)} %get-tuple-element.37), kind=kOutput, calls=%fused_computation.27 | convolution fusion | flops 2423390208 | bytes 12582916 | tf_op jit(solution)/shard_map/dot_general | solution.py:228
  87.5 1.7 collective-permute-done.10
  89.4 1.6 collective-permute-done.13
  93.4 14.9 %collective-permute-done.15 = bf16[128,3072]{1,0:T(8,128)(2,1)S(1)} collective-permute-done((bf16[128,3072]{1,0:T(8,128)(2,1)S(1)}, bf16[128,3072]{1,0:T(8,128)(2,1)S(1)}, u32[]{:S(2)}, u32[]{:S(2)}) %collective-permute-start.15) | collective-permute-done | bytes 786464 | tf_op jit(solution)/shard_map/ppermute | solution.py:213
  111.3 3.0 %fusion.23.refs_6_ = bf16[256,1536]{1,0:T(8,128)(2,1)S(1)} fusion(bf16[1024,1536]{1,0:T(8,128)(2,1)S(1)} %copy-done.7, s32[]{:T(128)S(6)} %select_n.224, bf16[3072,1536]{1,0:T(8,128)(2,1)S(1)} %bitcast.19, bf16[128,3072]{1,0:T(8,128)(2,1)S(1)} %get-tuple-element.36, bf16[128,3072]{1,0:T(8,128)(2,1)S(1)} %get-tuple-element.35), kind=kOutput, calls=%fused_computation.33 | convolution fusion | flops 2423390208 | bytes 12582916 | tf_op jit(solution)/shard_map/dot_general | solution.py:228
  115.8 3.0 %fusion.5.refs_7_ = bf16[256,1536]{1,0:T(8,128)(2,1)S(1)} fusion(bf16[1024,1536]{1,0:T(8,128)(2,1)S(1)} %copy-done.7, s32[]{:T(128)S(6)} %select_n.199, bf16[3072,1536]{1,0:T(8,128)(2,1)S(1)} %bitcast.19, bf16[128,3072]{1,0:T(8,128)(2,1)S(1)} %get-tuple-element.42, bf16[128,3072]{1,0:T(8,128)(2,1)S(1)} %get-tuple-element.41), kind=kOutput, calls=%fused_computation.15 | convolution fusion | flops 2423390208 | bytes 12582916 | tf_op jit(solution)/shard_map/dot_general | solution.py:228
  118.8 3.1 %shard_map.111 = bf16[768,768]{1,0:T(8,128)(2,1)S(1)} custom-call(s32[1]{0:T(128)} %bitcast.3.owners_ref, bf16[256,3072]{1,0:T(8,128)(2,1)S(1)} %get-tuple-element.50.refs_0_, bf16[256,3072]{1,0:T(8,128)(2,1)} %pad_maximum_fusion.2.refs_1_, bf16[256,3072]{1,0:T(8,128)(2,1)} %pad_maximum_fusion.3.refs_2_, bf16[256,3072]{1,0:T(8,128)(2,1)} %get-tuple-element.49.refs_3_, ...), custom_call_target="tpu_custom_call" | custom-call | flops 1207959552 | bytes 4325376 | tf_op jit(solution)/shard_map/pallas_call | solution.py:79
  123.6 2.9 %shard_map.107 = bf16[768,768]{1,0:T(8,128)(2,1)S(1)} custom-call(s32[1]{0:T(128)} %bitcast.3.owners_ref, bf16[256,3072]{1,0:T(8,128)(2,1)S(1)} %get-tuple-element.50.refs_0_, bf16[256,3072]{1,0:T(8,128)(2,1)} %pad_maximum_fusion.2.refs_1_, bf16[256,3072]{1,0:T(8,128)(2,1)} %pad_maximum_fusion.3.refs_2_, bf16[256,3072]{1,0:T(8,128)(2,1)} %get-tuple-element.49.refs_3_, ...), custom_call_target="tpu_custom_call" | custom-call | flops 1207959552 | bytes 4325376 | tf_op jit(solution)/shard_map/pallas_call | solution.py:79
  130.5 2.9 %shard_map.109 = bf16[768,768]{1,0:T(8,128)(2,1)S(1)} custom-call(s32[1]{0:T(128)} %bitcast.2.owners_ref, bf16[256,3072]{1,0:T(8,128)(2,1)S(1)} %get-tuple-element.50.refs_0_, bf16[256,3072]{1,0:T(8,128)(2,1)} %pad_maximum_fusion.2.refs_1_, bf16[256,3072]{1,0:T(8,128)(2,1)} %pad_maximum_fusion.3.refs_2_, bf16[256,3072]{1,0:T(8,128)(2,1)} %get-tuple-element.49.refs_3_, ...), custom_call_target="tpu_custom_call" | custom-call | flops 1207959552 | bytes 4325376 | tf_op jit(solution)/shard_map/pallas_call | solution.py:79
  133.4 2.9 %shard_map.106 = bf16[768,768]{1,0:T(8,128)(2,1)S(1)} custom-call(s32[1]{0:T(128)} %bitcast.2.owners_ref, bf16[256,3072]{1,0:T(8,128)(2,1)S(1)} %get-tuple-element.50.refs_0_, bf16[256,3072]{1,0:T(8,128)(2,1)} %pad_maximum_fusion.2.refs_1_, bf16[256,3072]{1,0:T(8,128)(2,1)} %pad_maximum_fusion.3.refs_2_, bf16[256,3072]{1,0:T(8,128)(2,1)} %get-tuple-element.49.refs_3_, ...), custom_call_target="tpu_custom_call" | custom-call | flops 1207959552 | bytes 4325376 | tf_op jit(solution)/shard_map/pallas_call | solution.py:79
  136.3 2.9 %shard_map.110 = bf16[768,768]{1,0:T(8,128)(2,1)S(1)} custom-call(s32[1]{0:T(128)} %bitcast.1.owners_ref, bf16[256,3072]{1,0:T(8,128)(2,1)S(1)} %get-tuple-element.50.refs_0_, bf16[256,3072]{1,0:T(8,128)(2,1)} %pad_maximum_fusion.2.refs_1_, bf16[256,3072]{1,0:T(8,128)(2,1)} %pad_maximum_fusion.3.refs_2_, bf16[256,3072]{1,0:T(8,128)(2,1)} %get-tuple-element.49.refs_3_, ...), custom_call_target="tpu_custom_call" | custom-call | flops 1207959552 | bytes 4325376 | tf_op jit(solution)/shard_map/pallas_call | solution.py:79
  139.3 2.9 %shard_map.105 = bf16[768,768]{1,0:T(8,128)(2,1)S(1)} custom-call(s32[1]{0:T(128)} %bitcast.1.owners_ref, bf16[256,3072]{1,0:T(8,128)(2,1)S(1)} %get-tuple-element.50.refs_0_, bf16[256,3072]{1,0:T(8,128)(2,1)} %pad_maximum_fusion.2.refs_1_, bf16[256,3072]{1,0:T(8,128)(2,1)} %pad_maximum_fusion.3.refs_2_, bf16[256,3072]{1,0:T(8,128)(2,1)} %get-tuple-element.49.refs_3_, ...), custom_call_target="tpu_custom_call" | custom-call | flops 1207959552 | bytes 4325376 | tf_op jit(solution)/shard_map/pallas_call | solution.py:79
  142.2 2.9 %shard_map.108.refs_3_ = bf16[768,768]{1,0:T(8,128)(2,1)S(1)} custom-call(s32[1]{0:T(128)} %bitcast.owners_ref.owner_ref, bf16[256,3072]{1,0:T(8,128)(2,1)S(1)} %get-tuple-element.50.refs_0_, bf16[256,3072]{1,0:T(8,128)(2,1)} %pad_maximum_fusion.2.refs_1_, bf16[256,3072]{1,0:T(8,128)(2,1)} %pad_maximum_fusion.3.refs_2_, ...), custom_call_target="tpu_custom_call" | custom-call | flops 1207959552 | bytes 4325376 | tf_op jit(solution)/shard_map/pallas_call | solution.py:79
  145.1 2.9 %shard_map.104.refs_0_ = bf16[768,768]{1,0:T(8,128)(2,1)S(1)} custom-call(s32[1]{0:T(128)} %bitcast.owners_ref.owner_ref, bf16[256,3072]{1,0:T(8,128)(2,1)S(1)} %get-tuple-element.50.refs_0_, bf16[256,3072]{1,0:T(8,128)(2,1)} %pad_maximum_fusion.2.refs_1_, bf16[256,3072]{1,0:T(8,128)(2,1)} %pad_maximum_fusion.3.refs_2_, ...), custom_call_target="tpu_custom_call" | custom-call | flops 1207959552 | bytes 4325376 | tf_op jit(solution)/shard_map/pallas_call | solution.py:79
  148.0 2.9 %collective-permute-done.30 = bf16[768,768]{1,0:T(8,128)(2,1)} collective-permute-done((bf16[768,768]{1,0:T(8,128)(2,1)S(1)}, bf16[768,768]{1,0:T(8,128)(2,1)}, u32[]{:S(2)}, u32[]{:S(2)}) %collective-permute-start.30) | collective-permute-done | bytes 1179680 | tf_op jit(solution)/shard_map/ppermute | solution.py:40
  153.9 9.9 %collective-permute-done.17 = bf16[256,768]{1,0:T(8,128)(2,1)} collective-permute-done((bf16[256,768]{1,0:T(8,128)(2,1)}, bf16[256,768]{1,0:T(8,128)(2,1)}, u32[]{:S(2)}, u32[]{:S(2)}) %collective-permute-start.17) | collective-permute-done | bytes 393248 | tf_op jit(solution)/shard_map/ppermute | solution.py:40
  165.9 2.6 %add_convert_fusion.1 = bf16[768,768]{1,0:T(8,128)(2,1)} fusion(bf16[768,768]{1,0:T(8,128)(2,1)} %collective-permute-done.27, bf16[768,768]{1,0:T(8,128)(2,1)S(1)} %shard_map.106), kind=kLoop, calls=%fused_computation.9 | loop fusion | flops 2359296 | bytes 3538944 | tf_op jit(solution)/shard_map/convert_element_type | solution.py:57
  170.5 1.6 collective-permute-done.18
  173.7 27.7 %collective-permute-done.21 = bf16[256,768]{1,0:T(8,128)(2,1)S(1)} collective-permute-done((bf16[256,768]{1,0:T(8,128)(2,1)}, bf16[256,768]{1,0:T(8,128)(2,1)S(1)}, u32[]{:S(2)}, u32[]{:S(2)}) %collective-permute-start.21) | collective-permute-done | bytes 393248 | tf_op jit(solution)/shard_map/ppermute | solution.py:40
  205.0 25.4 %collective-permute-done.22 = bf16[256,768]{1,0:T(8,128)(2,1)S(1)} collective-permute-done((bf16[256,768]{1,0:T(8,128)(2,1)}, bf16[256,768]{1,0:T(8,128)(2,1)S(1)}, u32[]{:S(2)}, u32[]{:S(2)}) %collective-permute-start.22) | collective-permute-done | bytes 393248 | tf_op jit(solution)/shard_map/ppermute | solution.py:40
  230.5 8.1 %shard_map.103.curv_ref = f32[768,1536]{1,0:T(8,128)} custom-call(bf16[768,1536]{1,0:T(8,128)(2,1)} %probes_ref.1, f32[768,1536]{1,0:T(8,128)} %curv_ref.1, bf16[256,768]{1,0:T(8,128)(2,1)S(1)} %get-tuple-element.18.refs_0_, bf16[256,768]{1,0:T(8,128)(2,1)S(1)} %collective-permute-done.5.refs_1_, bf16[256,768]{1,0:T(8,128)(2,1)S(1)} %collective-permute-done.6.refs_2_, ...), custom_call_target="tpu_custom_call" | custom-call | flops 2415919104 | bytes 14155776 | tf_op jit(solution)/shard_map/pallas_call | solution.py:112
  239.7 9.3 %shard_map.112 = (bf16[768,1536]{1,0:T(8,128)(2,1)}, f32[768,1536]{1,0:T(8,128)}) custom-call(s32[1]{0:T(128)} %bitcast.owners_ref.owner_ref, bf16[3072,1536]{1,0:T(8,128)(2,1)} %weight_ref.1, f32[768,1536]{1,0:T(8,128)} %mom_ref.1, f32[768,1536]{1,0:T(8,128)} %shard_map.103.curv_ref, bf16[768,768]{1,0:T(8,128)(2,1)S(1)} %shard_map.104.refs_0_, ...), custom_call_target="tpu_custom_call" | custom-call | flops 11796480 | bytes 25952256 | tf_op jit(solution)/shard_map/pallas_call | solution.py:150
  (108 shorter events, 47.8 us)
Async XLA Ops:
  0.7 12.5 %collective-permute-start.1 = (bf16[32,3072]{1,0:T(8,128)(2,1)}, bf16[32,3072]{1,0:T(8,128)(2,1)S(1)}, u32[]{:S(2)}, u32[]{:S(2)}) collective-permute-start(bf16[32,3072]{1,0:T(8,128)(2,1)} %param.9), channel_id=1, source_target_pairs={{0,2},{1,3},{2,0},{3,1},{4,6},{5,7},{6,4},{7,5},{8,10},{9,11},{10,... | collective-permute-start | bytes 589832 | tf_op jit(solution)/shard_map/ppermute | solution.py:40
  3.7 34.4 %collective-permute-start.2 = (bf16[32,3072]{1,0:T(8,128)(2,1)}, bf16[32,3072]{1,0:T(8,128)(2,1)}, u32[]{:S(2)}, u32[]{:S(2)}) collective-permute-start(bf16[32,3072]{1,0:T(8,128)(2,1)} %param.9), channel_id=1, source_target_pairs={{0,4},{1,5},{2,6},{3,7},{4,0},{5,1},{6,2},{7,3},{8,12},{9,13},{10,... | collective-permute-start | bytes 589832 | tf_op jit(solution)/shard_map/ppermute | solution.py:40
  6.3 31.8 %collective-permute-start.3 = (bf16[32,3072]{1,0:T(8,128)(2,1)}, bf16[32,3072]{1,0:T(8,128)(2,1)}, u32[]{:S(2)}, u32[]{:S(2)}) collective-permute-start(bf16[32,3072]{1,0:T(8,128)(2,1)} %param.9), channel_id=1, source_target_pairs={{0,6},{1,7},{2,4},{3,5},{4,2},{5,3},{6,0},{7,1},{8,14},{9,15},{10,... | collective-permute-start | bytes 589832 | tf_op jit(solution)/shard_map/ppermute | solution.py:40
  6.3 44.2 %collective-permute-start = (bf16[128,3072]{1,0:T(8,128)(2,1)}, bf16[128,3072]{1,0:T(8,128)(2,1)}, u32[]{:S(2)}, u32[]{:S(2)}) collective-permute-start(bf16[128,3072]{1,0:T(8,128)(2,1)} %param.8), channel_id=1, source_target_pairs={{0,4},{1,5},{2,0},{3,1},{4,6},{5,7},{6,2},{7,3},{8,12},{9,13},{10,... | collective-permute-start | bytes 2359304 | tf_op jit(solution)/shard_map/ppermute | solution.py:213
  8.2 33.0 %collective-permute-start.23 = (bf16[128,3072]{1,0:T(8,128)(2,1)}, bf16[128,3072]{1,0:T(8,128)(2,1)}, u32[]{:S(2)}, u32[]{:S(2)}) collective-permute-start(bf16[128,3072]{1,0:T(8,128)(2,1)} %param.8), channel_id=1, source_target_pairs={{0,1},{1,0},{2,3},{3,2},{4,5},{5,4},{6,7},{7,6},{8,9},{9,8},{10,11... | collective-permute-start | bytes 2359304 | tf_op jit(solution)/shard_map/ppermute | solution.py:40
  39.2 11.1 %collective-permute-start.4 = (bf16[128,3072]{1,0:T(8,128)(2,1)S(1)}, bf16[128,3072]{1,0:T(8,128)(2,1)S(1)}, u32[]{:S(2)}, u32[]{:S(2)}) collective-permute-start(bf16[128,3072]{1,0:T(8,128)(2,1)S(1)} %pad_maximum_fusion.4), channel_id=1, source_target_pairs={{0,1},{1,0},{2,3},{3,2},{4,5},{5,4},{6,7},{7,6},{8,9},{9,8},{10,11... | collective-permute-start | bytes 2359304 | tf_op jit(solution)/shard_map/ppermute | solution.py:40
  50.6 26.8 %collective-permute-start.8 = (bf16[128,3072]{1,0:T(8,128)(2,1)}, bf16[128,3072]{1,0:T(8,128)(2,1)S(1)}, u32[]{:S(2)}, u32[]{:S(2)}) collective-permute-start(bf16[128,3072]{1,0:T(8,128)(2,1)} %collective-permute-done), channel_id=1, source_target_pairs={{0,4},{1,5},{2,0},{3,1},{4,6},{5,7},{6,2},{7,3},{8,12},{9,13},{10,... | collective-permute-start | bytes 2359304 | tf_op jit(solution)/shard_map/ppermute | solution.py:213
  55.0 25.6 %collective-permute-start.24 = (bf16[128,3072]{1,0:T(8,128)(2,1)}, bf16[128,3072]{1,0:T(8,128)(2,1)S(1)}, u32[]{:S(2)}, u32[]{:S(2)}) collective-permute-start(bf16[128,3072]{1,0:T(8,128)(2,1)} %collective-permute-done), channel_id=1, source_target_pairs={{0,1},{1,0},{2,3},{3,2},{4,5},{5,4},{6,7},{7,6},{8,9},{9,8},{10,11... | collective-permute-start | bytes 2359304 | tf_op jit(solution)/shard_map/ppermute | solution.py:40
  55.2 12.9 %collective-permute-start.7 = (bf16[256,768]{1,0:T(8,128)(2,1)S(1)}, bf16[256,768]{1,0:T(8,128)(2,1)S(1)}, u32[]{:S(2)}, u32[]{:S(2)}) collective-permute-start(bf16[256,768]{1,0:T(8,128)(2,1)S(1)} %get-tuple-element.21), channel_id=1, source_target_pairs={{0,24},{8,16},{16,8},{24,0},{1,25},{9,17},{17,9},{25,1},{2,26},{10... | collective-permute-start | bytes 1179656 | tf_op jit(solution)/shard_map/ppermute | solution.py:40
  60.2 15.7 %collective-permute-start.6 = (bf16[256,768]{1,0:T(8,128)(2,1)S(1)}, bf16[256,768]{1,0:T(8,128)(2,1)S(1)}, u32[]{:S(2)}, u32[]{:S(2)}) collective-permute-start(bf16[256,768]{1,0:T(8,128)(2,1)S(1)} %get-tuple-element.20), channel_id=1, source_target_pairs={{0,16},{8,24},{16,0},{24,8},{1,17},{9,25},{17,1},{25,9},{2,18},{10... | collective-permute-start | bytes 1179656 | tf_op jit(solution)/shard_map/ppermute | solution.py:40
  60.8 15.9 %collective-permute-start.5 = (bf16[256,768]{1,0:T(8,128)(2,1)S(1)}, bf16[256,768]{1,0:T(8,128)(2,1)S(1)}, u32[]{:S(2)}, u32[]{:S(2)}) collective-permute-start(bf16[256,768]{1,0:T(8,128)(2,1)S(1)} %get-tuple-element.19), channel_id=1, source_target_pairs={{0,8},{8,0},{16,24},{24,16},{1,9},{9,1},{17,25},{25,17},{2,10},{10... | collective-permute-start | bytes 1179656 | tf_op jit(solution)/shard_map/ppermute | solution.py:40
  77.4 15.2 %collective-permute-start.25 = (bf16[128,3072]{1,0:T(8,128)(2,1)S(1)}, bf16[128,3072]{1,0:T(8,128)(2,1)S(1)}, u32[]{:S(2)}, u32[]{:S(2)}) collective-permute-start(bf16[128,3072]{1,0:T(8,128)(2,1)S(1)} %collective-permute-done.8), channel_id=1, source_target_pairs={{0,1},{1,0},{2,3},{3,2},{4,5},{5,4},{6,7},{7,6},{8,9},{9,8},{10,11... | collective-permute-start | bytes 2359304 | tf_op jit(solution)/shard_map/ppermute | solution.py:40
  77.6 11.6 %collective-permute-start.10 = (bf16[256,768]{1,0:T(8,128)(2,1)S(1)}, bf16[256,768]{1,0:T(8,128)(2,1)S(1)}, u32[]{:S(2)}, u32[]{:S(2)}) collective-permute-start(bf16[256,768]{1,0:T(8,128)(2,1)S(1)} %get-tuple-element.48), channel_id=1, source_target_pairs={{0,8},{8,0},{16,24},{24,16},{1,9},{9,1},{17,25},{25,17},{2,10},{10... | collective-permute-start | bytes 1179656 | tf_op jit(solution)/shard_map/ppermute | solution.py:40
  79.1 12.0 %collective-permute-start.13 = (bf16[256,768]{1,0:T(8,128)(2,1)S(1)}, bf16[256,768]{1,0:T(8,128)(2,1)S(1)}, u32[]{:S(2)}, u32[]{:S(2)}) collective-permute-start(bf16[256,768]{1,0:T(8,128)(2,1)S(1)} %get-tuple-element.47), channel_id=1, source_target_pairs={{0,16},{8,24},{16,0},{24,8},{1,17},{9,25},{17,1},{25,9},{2,18},{10... | collective-permute-start | bytes 1179656 | tf_op jit(solution)/shard_map/ppermute | solution.py:40
  86.2 23.3 %collective-permute-start.12 = (bf16[256,768]{1,0:T(8,128)(2,1)S(1)}, bf16[256,768]{1,0:T(8,128)(2,1)S(1)}, u32[]{:S(2)}, u32[]{:S(2)}) collective-permute-start(bf16[256,768]{1,0:T(8,128)(2,1)S(1)} %slice.45), channel_id=1, source_target_pairs={{0,16},{8,24},{16,0},{24,8},{1,17},{9,25},{17,1},{25,9},{2,18},{10... | collective-permute-start | bytes 1179656 | tf_op jit(solution)/shard_map/ppermute | solution.py:40
  86.8 22.7 %collective-permute-start.9 = (bf16[256,768]{1,0:T(8,128)(2,1)S(1)}, bf16[256,768]{1,0:T(8,128)(2,1)S(1)}, u32[]{:S(2)}, u32[]{:S(2)}) collective-permute-start(bf16[256,768]{1,0:T(8,128)(2,1)S(1)} %slice.39), channel_id=1, source_target_pairs={{0,8},{8,0},{16,24},{24,16},{1,9},{9,1},{17,25},{25,17},{2,10},{10... | collective-permute-start | bytes 1179656 | tf_op jit(solution)/shard_map/ppermute | solution.py:40
  89.2 19.2 %collective-permute-start.15 = (bf16[128,3072]{1,0:T(8,128)(2,1)S(1)}, bf16[128,3072]{1,0:T(8,128)(2,1)S(1)}, u32[]{:S(2)}, u32[]{:S(2)}) collective-permute-start(bf16[128,3072]{1,0:T(8,128)(2,1)S(1)} %collective-permute-done.8), channel_id=1, source_target_pairs={{0,4},{1,5},{2,0},{3,1},{4,6},{5,7},{6,2},{7,3},{8,12},{9,13},{10,... | collective-permute-start | bytes 2359304 | tf_op jit(solution)/shard_map/ppermute | solution.py:213
  91.0 18.5 %collective-permute-start.11 = (bf16[256,768]{1,0:T(8,128)(2,1)S(1)}, bf16[256,768]{1,0:T(8,128)(2,1)S(1)}, u32[]{:S(2)}, u32[]{:S(2)}) collective-permute-start(bf16[256,768]{1,0:T(8,128)(2,1)S(1)} %add_convert_fusion.3), channel_id=1, source_target_pairs={{0,16},{8,24},{16,0},{24,8},{1,17},{9,25},{17,1},{25,9},{2,18},{10... | collective-permute-start | bytes 1179656 | tf_op jit(solution)/shard_map/ppermute | solution.py:40
  92.7 16.9 %collective-permute-start.14 = (bf16[256,768]{1,0:T(8,128)(2,1)S(1)}, bf16[256,768]{1,0:T(8,128)(2,1)S(1)}, u32[]{:S(2)}, u32[]{:S(2)}) collective-permute-start(bf16[256,768]{1,0:T(8,128)(2,1)S(1)} %add_convert_fusion.2), channel_id=1, source_target_pairs={{0,8},{8,0},{16,24},{24,16},{1,9},{9,1},{17,25},{25,17},{2,10},{10... | collective-permute-start | bytes 1179656 | tf_op jit(solution)/shard_map/ppermute | solution.py:40
  108.3 6.0 %collective-permute-start.16 = (bf16[128,3072]{1,0:T(8,128)(2,1)S(1)}, bf16[128,3072]{1,0:T(8,128)(2,1)S(1)}, u32[]{:S(2)}, u32[]{:S(2)}) collective-permute-start(bf16[128,3072]{1,0:T(8,128)(2,1)S(1)} %collective-permute-done.15), channel_id=1, source_target_pairs={{0,1},{1,0},{2,3},{3,2},{4,5},{5,4},{6,7},{7,6},{8,9},{9,8},{10,11... | collective-permute-start | bytes 2359304 | tf_op jit(solution)/shard_map/ppermute | solution.py:40
  122.0 28.9 %collective-permute-start.30 = (bf16[768,768]{1,0:T(8,128)(2,1)S(1)}, bf16[768,768]{1,0:T(8,128)(2,1)}, u32[]{:S(2)}, u32[]{:S(2)}) collective-permute-start(bf16[768,768]{1,0:T(8,128)(2,1)S(1)} %shard_map.111), channel_id=1, source_target_pairs={{0,16},{8,24},{16,0},{24,8},{1,17},{9,25},{17,1},{25,9},{2,18},{10... | collective-permute-start | bytes 3538952 | tf_op jit(solution)/shard_map/ppermute | solution.py:40
  126.4 37.9 %collective-permute-start.27 = (bf16[768,768]{1,0:T(8,128)(2,1)S(1)}, bf16[768,768]{1,0:T(8,128)(2,1)}, u32[]{:S(2)}, u32[]{:S(2)}) collective-permute-start(bf16[768,768]{1,0:T(8,128)(2,1)S(1)} %shard_map.107), channel_id=1, source_target_pairs={{0,8},{8,0},{16,24},{24,16},{1,9},{9,1},{17,25},{25,17},{2,10},{10... | collective-permute-start | bytes 3538952 | tf_op jit(solution)/shard_map/ppermute | solution.py:40
  127.9 35.9 %collective-permute-start.17 = (bf16[256,768]{1,0:T(8,128)(2,1)}, bf16[256,768]{1,0:T(8,128)(2,1)}, u32[]{:S(2)}, u32[]{:S(2)}) collective-permute-start(bf16[256,768]{1,0:T(8,128)(2,1)} %get-tuple-element.27), channel_id=1, source_target_pairs={{0,8},{8,0},{16,24},{24,16},{1,9},{9,1},{17,25},{25,17},{2,10},{10... | collective-permute-start | bytes 1179656 | tf_op jit(solution)/shard_map/ppermute | solution.py:40
  128.5 41.4 %collective-permute-start.19 = (bf16[256,768]{1,0:T(8,128)(2,1)}, bf16[256,768]{1,0:T(8,128)(2,1)}, u32[]{:S(2)}, u32[]{:S(2)}) collective-permute-start(bf16[256,768]{1,0:T(8,128)(2,1)} %get-tuple-element.27), channel_id=1, source_target_pairs={{0,16},{8,24},{16,0},{24,8},{1,17},{9,25},{17,1},{25,9},{2,18},{10... | collective-permute-start | bytes 1179656 | tf_op jit(solution)/shard_map/ppermute | solution.py:40
  129.0 39.4 %collective-permute-start.20 = (bf16[256,768]{1,0:T(8,128)(2,1)S(1)}, bf16[256,768]{1,0:T(8,128)(2,1)}, u32[]{:S(2)}, u32[]{:S(2)}) collective-permute-start(bf16[256,768]{1,0:T(8,128)(2,1)S(1)} %get-tuple-element.28), channel_id=1, source_target_pairs={{0,16},{8,24},{16,0},{24,8},{1,17},{9,25},{17,1},{25,9},{2,18},{10... | collective-permute-start | bytes 1179656 | tf_op jit(solution)/shard_map/ppermute | solution.py:40
  150.9 21.2 %collective-permute-start.18 = (bf16[256,768]{1,0:T(8,128)(2,1)S(1)}, bf16[256,768]{1,0:T(8,128)(2,1)S(1)}, u32[]{:S(2)}, u32[]{:S(2)}) collective-permute-start(bf16[256,768]{1,0:T(8,128)(2,1)S(1)} %get-tuple-element.28), channel_id=1, source_target_pairs={{0,8},{8,0},{16,24},{24,16},{1,9},{9,1},{17,25},{25,17},{2,10},{10... | collective-permute-start | bytes 1179656 | tf_op jit(solution)/shard_map/ppermute | solution.py:40
  163.8 74.8 %collective-permute-start.29 = (bf16[768,768]{1,0:T(8,128)(2,1)S(1)}, bf16[768,768]{1,0:T(8,128)(2,1)S(1)}, u32[]{:S(2)}, u32[]{:S(2)}) collective-permute-start(bf16[768,768]{1,0:T(8,128)(2,1)S(1)} %shard_map.109), channel_id=1, source_target_pairs={{0,16},{8,24},{16,0},{24,8},{1,17},{9,25},{17,1},{25,9},{2,18},{10... | collective-permute-start | bytes 3538952 | tf_op jit(solution)/shard_map/ppermute | solution.py:40
  164.3 37.0 %collective-permute-start.21 = (bf16[256,768]{1,0:T(8,128)(2,1)}, bf16[256,768]{1,0:T(8,128)(2,1)S(1)}, u32[]{:S(2)}, u32[]{:S(2)}) collective-permute-start(bf16[256,768]{1,0:T(8,128)(2,1)} %collective-permute-done.17), channel_id=1, source_target_pairs={{0,16},{8,24},{16,0},{24,8},{1,17},{9,25},{17,1},{25,9},{2,18},{10... | collective-permute-start | bytes 1179656 | tf_op jit(solution)/shard_map/ppermute | solution.py:40
  168.5 70.1 %collective-permute-start.26 = (bf16[768,768]{1,0:T(8,128)(2,1)S(1)}, bf16[768,768]{1,0:T(8,128)(2,1)S(1)}, u32[]{:S(2)}, u32[]{:S(2)}) collective-permute-start(bf16[768,768]{1,0:T(8,128)(2,1)S(1)} %shard_map.105), channel_id=1, source_target_pairs={{0,8},{8,0},{16,24},{24,16},{1,9},{9,1},{17,25},{25,17},{2,10},{10... | collective-permute-start | bytes 3538952 | tf_op jit(solution)/shard_map/ppermute | solution.py:40
  169.9 68.7 %collective-permute-start.31 = (bf16[768,768]{1,0:T(8,128)(2,1)S(1)}, bf16[768,768]{1,0:T(8,128)(2,1)S(1)}, u32[]{:S(2)}, u32[]{:S(2)}) collective-permute-start(bf16[768,768]{1,0:T(8,128)(2,1)S(1)} %add_convert_fusion), channel_id=1, source_target_pairs={{0,8},{8,0},{16,24},{24,16},{1,9},{9,1},{17,25},{25,17},{2,10},{10... | collective-permute-start | bytes 3538952 | tf_op jit(solution)/shard_map/ppermute | solution.py:40
  172.1 66.5 %collective-permute-start.28 = (bf16[768,768]{1,0:T(8,128)(2,1)}, bf16[768,768]{1,0:T(8,128)(2,1)S(1)}, u32[]{:S(2)}, u32[]{:S(2)}) collective-permute-start(bf16[768,768]{1,0:T(8,128)(2,1)} %add_convert_fusion.1), channel_id=1, source_target_pairs={{0,16},{8,24},{16,0},{24,8},{1,17},{9,25},{17,1},{25,9},{2,18},{10... | collective-permute-start | bytes 3538952 | tf_op jit(solution)/shard_map/ppermute | solution.py:40
  201.4 29.1 %collective-permute-start.22 = (bf16[256,768]{1,0:T(8,128)(2,1)}, bf16[256,768]{1,0:T(8,128)(2,1)S(1)}, u32[]{:S(2)}, u32[]{:S(2)}) collective-permute-start(bf16[256,768]{1,0:T(8,128)(2,1)} %collective-permute-done.20), channel_id=1, source_target_pairs={{0,8},{8,0},{16,24},{24,16},{1,9},{9,1},{17,25},{25,17},{2,10},{10... | collective-permute-start | bytes 1179656 | tf_op jit(solution)/shard_map/ppermute | solution.py:40
  (11 other events, 167.9 us)
